TPU v7x, 32 devices: a whole 2x2x4 slice. The times are simulated.
32 devices in a mesh: seq: 16 (over z, y, core), head: 2 (over x).
Axes of the slice: x: 2, y: 2, z: 4, core: 2. Of those that a mesh axis runs over, the one named last changes fastest.
Arguments:
- xin: bfloat16 [8192, 8192], P('seq', 'head'), may hold values from -6 to 6
- gate_z: bfloat16 [8192, 8192], P('seq', 'head'), may hold values from -6 to 6
- b_proj: bfloat16 [8192, 8, 256], P('seq', 'head'), may hold values from -0.375 to 0.375
- c_proj: bfloat16 [8192, 8, 256], P('seq', 'head'), may hold values from -0.375 to 0.375
- log_retain: float32 [8192, 128], P('seq', 'head'), may hold values from -2 to 0, as said below
- skip_d: float32 [128], P('head'), may hold values from 0.5 to 2
- norm_gain: float32 [8192], P('head'), may hold values from 0.5 to 1.5
- w_out: bfloat16 [8192, 4096], P('head', 'seq'), may hold values from -0.0625 to 0.0625
- residual: bfloat16 [8192, 4096], P(('seq', 'head')), may hold values from -24 to 24
- refusal: float32 [4096], replicated, may hold values from -6 to 6
- stream_gain: float32 [4096], replicated, may hold values from 0.5 to 1.5
- w_in: bfloat16 [4096, 8192], P('seq', 'head'), may hold values from -0.09375 to 0.09375
Outputs:
- stream: bfloat16 [8192, 4096], P(('seq', 'head'))
- next_x: bfloat16 [8192, 8192], P('seq', 'head')
Inputs may be any that keep to these rules, and one draw needn't show every extreme that they name: `log_retain`: every entry is negative.
All inputs are finite; a program needn't handle non-finite values.
Results may differ from a plain program's by a relative error of at most 0.02.
Values may be sent and summed in bfloat16 or wider, within the bound.
A program may use at most 256 MiB of HBM per device.

v0:
```python
import jax
import jax.numpy as jnp
from jax import lax
from jax.sharding import PartitionSpec as P

SPAN = 256


def prefix(array, axis, combine, identity):
    devices, place = (lax.axis_size(axis), lax.axis_index(axis))
    everything = jax.tree.map(
        lambda part, kind: lax.all_gather(part.astype(kind), axis),
        array,
        (jnp.bfloat16, jnp.bfloat16),
    )
    start = jax.tree.map(
        lambda part, zero: jnp.broadcast_to(jnp.asarray(zero, part.dtype), part.shape),
        array,
        identity,
    )

    def turn(k, before):
        reached = k < place
        new = combine(
            before, jax.tree.map(lambda part, own: part[k].astype(own.dtype), everything, array)
        )
        return jax.tree.map(lambda a, b: jnp.where(reached, a, b), new, before)

    return lax.fori_loop(0, devices, turn, start)


def carry_combine(earlier, later):
    decay_early, state_early = earlier
    decay_later, state_later = later
    return (
        decay_early + decay_later,
        jnp.exp(decay_later)[:, None, None] * state_early + state_later,
    )


def body(
    xin,
    gate_z,
    b_proj,
    c_proj,
    log_retain,
    skip_d,
    norm_gain,
    w_out,
    residual,
    refusal,
    stream_gain,
    w_in,
):
    seq_rows, channels = xin.shape
    head_count = log_retain.shape[1]
    head_width = channels // head_count
    group_count = b_proj.shape[1]
    state_width = b_proj.shape[2]
    per_group = head_count // group_count
    block_count = seq_rows // SPAN
    inputs = xin.reshape(block_count, SPAN, head_count, head_width)
    b_grouped = b_proj.reshape(block_count, SPAN, group_count, state_width)
    c_grouped = c_proj.reshape(block_count, SPAN, group_count, state_width)
    scores = jnp.einsum("klgn,ksgn->kgls", c_grouped, b_grouped, preferred_element_type=jnp.float32)
    scores = jnp.repeat(scores, per_group, axis=1)
    cum = jnp.cumsum(log_retain.reshape(block_count, SPAN, head_count), axis=1)
    cum_heads = jnp.transpose(cum, (0, 2, 1))
    later_pos = lax.broadcasted_iota(jnp.int32, (SPAN, SPAN), 0)
    earlier_pos = lax.broadcasted_iota(jnp.int32, (SPAN, SPAN), 1)
    causal = later_pos >= earlier_pos
    gap = cum_heads[:, :, :, None] - cum_heads[:, :, None, :]
    mixing = (jnp.where(causal, jnp.exp(jnp.where(causal, gap, 0.0)), 0.0) * scores).astype(
        jnp.bfloat16
    )
    intra = jnp.einsum("khls,kshp->klhp", mixing, inputs, preferred_element_type=jnp.float32)
    tail_decay = jnp.exp(cum_heads[:, :, -1:] - cum_heads)
    b_heads = jnp.repeat(b_grouped, per_group, axis=2)
    weighted_b = (
        b_heads.astype(jnp.float32) * jnp.transpose(tail_decay, (0, 2, 1))[..., None]
    ).astype(jnp.bfloat16)
    block_state = jnp.einsum(
        "klhn,klhp->khnp", weighted_b, inputs, preferred_element_type=jnp.float32
    )
    block_decay = cum_heads[:, :, -1]

    def advance(carried_state, pair):
        decay_here, state_here = pair
        return (jnp.exp(decay_here)[:, None, None] * carried_state + state_here, carried_state)

    zero_state = jnp.zeros((head_count, state_width, head_width), jnp.float32)
    device_state, local_starts = lax.scan(advance, zero_state, (block_decay, block_state))
    device_decay = jnp.sum(block_decay, axis=0)
    zero_decay = jnp.zeros((head_count,), jnp.float32)
    total_decay, incoming = prefix(
        (device_decay, device_state), "seq", carry_combine, (zero_decay, zero_state)
    )
    before_block = jnp.cumsum(block_decay, axis=0) - block_decay
    starts = local_starts + jnp.exp(before_block)[:, :, None, None] * incoming[None]
    c_heads = jnp.repeat(c_grouped, per_group, axis=2).astype(jnp.float32)
    carried = jnp.einsum("klhn,khnp->klhp", c_heads, starts, precision=lax.Precision.HIGHEST)
    carried = carried * jnp.exp(cum)[..., None]
    mixed = intra + carried + skip_d[None, None, :, None] * inputs.astype(jnp.float32)
    gated = mixed * jax.nn.silu(
        gate_z.reshape(block_count, SPAN, head_count, head_width).astype(jnp.float32)
    )
    grouped = gated.reshape(seq_rows, group_count, per_group * head_width)
    grouped = grouped * lax.rsqrt(jnp.mean(grouped * grouped, axis=-1, keepdims=True) + 1e-05)
    ssd_out = (grouped.reshape(seq_rows, channels) * norm_gain[None, :]).astype(jnp.bfloat16)
    partial_sum = jnp.dot(
        ssd_out,
        lax.all_gather(w_out, "seq", axis=1, tiled=True),
        preferred_element_type=jnp.float32,
    )
    mixer_out = lax.psum_scatter(
        partial_sum.astype(jnp.bfloat16), "head", scatter_dimension=0, tiled=True
    ).astype(jnp.float32)
    unit = refusal / jnp.sqrt(jnp.sum(refusal * refusal) + 1e-06)
    hidden = residual.astype(jnp.float32) + mixer_out
    coef = jnp.dot(hidden, unit, precision=lax.Precision.HIGHEST)
    stream = (hidden - coef[:, None] * unit[None, :]).astype(jnp.bfloat16)
    stream_float = stream.astype(jnp.float32)
    normed = (
        stream_float
        * lax.rsqrt(jnp.mean(stream_float * stream_float, axis=-1, keepdims=True) + 1e-05)
        * stream_gain[None, :]
    ).astype(jnp.bfloat16)
    all_rows = lax.all_gather(normed, "head", axis=0, tiled=True)
    next_float = jnp.dot(
        all_rows,
        lax.all_gather(w_in, "seq", axis=0, tiled=True),
        preferred_element_type=jnp.float32,
    )
    return (stream, next_float.astype(jnp.bfloat16))


def solution(mesh):
    in_specs = (
        P("seq", "head"),
        P("seq", "head"),
        P("seq", "head", None),
        P("seq", "head", None),
        P("seq", "head"),
        P("head"),
        P("head"),
        P("head", "seq"),
        P(("seq", "head"), None),
        P(),
        P(),
        P("seq", "head"),
    )
    out_specs = (P(("seq", "head"), None), P("seq", "head"))
    return jax.shard_map(body, mesh=mesh, in_specs=in_specs, out_specs=out_specs, check_vma=False)
```

profile of v0, /device:TPU:0, one launch (start us, length us, event | category | flops | bytes accessed | tf_op | source)
XLA Modules:
  0.0 944.0 jit_solution(13751169380933610521)
XLA Ops:
  12.1 12.5 %reshape.149 = bf16[2,256,64,64]{3,2,1,0:T(8,128)(2,1)} reshape(bf16[512,4096]{1,0:T(8,128)(2,1)} %param.16) | data formatting | bytes 8388608 | tf_op jit(solution)/shard_map/reshape | solution.py:62
  24.7 10.5 %copy.64 = bf16[2,256,64,64]{1,3,2,0:T(8,128)(2,1)} copy(bf16[2,256,64,64]{3,2,1,0:T(8,128)(2,1)} %reshape.149) | data formatting | bytes 8388608 | tf_op jit(solution)/shard_map/reshape | solution.py:62
  35.1 11.1 %broadcast_in_dim.53 = f32[2,256,4,16,256]{4,1,3,2,0:T(8,128)} broadcast(f32[2,256,4,256]{3,1,2,0:T(8,128)S(1)} %copy.65), dimensions={0,1,2,4} | broadcast | bytes 35651584 | tf_op jit(solution)/shard_map/broadcast_in_dim | solution.py:78
  46.3 22.1 %fusion.3 = f32[2,64,256,64]{3,2,1,0:T(8,128)} fusion(bf16[2,256,64,64]{1,3,2,0:T(8,128)(2,1)} %copy.64, f32[2,256,64,256]{3,1,2,0:T(8,128)} %bitcast.85, f32[2,256,64]{1,2,0:T(8,128)S(1)} %get-tuple-element.213), kind=kOutput, calls=%fused_computation.11 | convolution fusion | flops 1090519040 | bytes 46268416 | tf_op jit(solution)/shard_map/klhn,klhp->khnp/dot_general | solution.py:82
  68.4 33.1 %while.27 = (s32[]{:T(128)}, f32[64,256,64]{2,1,0:T(8,128)}, f32[2,64,256,64]{3,2,1,0:T(8,128)}, f32[2,64]{1,0:T(2,128)S(1)}, f32[2,64,256,64]{3,2,1,0:T(8,128)}, /*index=5*/s32[]{:T(128)}, s32[]{:T(128)}) while((s32[]{:T(128)}, f32[64,256,64]{2,1,0:T(8,128)}, f32[2,64,256,64]{3,2,1,0:T(8,128)}, f32[2,64]{1,0:T(2,128)S(1)}, ...), condition=%wide.region_3.4_spmd.clone, body=%wide.region_2.3_spmd.clone.sunk | while | flops 4194307 | bytes 29361504 | solution.py:92
  68.4 4.2 bitcast_dynamic-update-slice_fusion.2
  72.6 9.3 bitcast_add_fusion.2
  82.0 7.7 bitcast_dynamic-update-slice_fusion.2
  89.7 11.7 %bitcast_add_fusion.2 = f32[64,256,64]{2,1,0:T(8,128)} fusion(f32[2,64,256,64]{3,2,1,0:T(8,128)} %get-tuple-element.296, s32[]{:T(128)} %get-tuple-element.285, f32[64,256,64]{2,1,0:T(8,128)} %get-tuple-element.286, f32[64]{0:T(128)S(1)} %fusion.35, pred[]{:T(512)S(6)} %compare.6), kind=kLoop, calls=%fused_computation.1.clone.1 | loop fusion | flops 3145728 | bytes 12583173 | tf_op jit(solution)/shard_map/while/body/eval_jaxpr/add | solution.py:89
  101.4 5.8 copy.68
  109.6 36.0 %all-reduce = bf16[1024]{0:T(1024)(128)(2,1)S(1)} all-reduce(bf16[1024]{0:T(1024)(128)(2,1)S(1)} %dynamic-update-slice), channel_id=2, replica_groups=mesh['seq'=16,'head'=2] {'seq'}, use_global_device_ids=true, to_apply=%add | all-reduce | flops 1024 | bytes 4096
  145.8 12.7 %reshape.150 = f32[2,256,64,64]{3,2,1,0:T(8,128)} reshape(bf16[512,4096]{1,0:T(8,128)(2,1)} %param.17) | data formatting | bytes 12582912 | tf_op jit(solution)/shard_map/convert_element_type | solution.py:105
  158.5 14.5 %copy.75 = f32[2,256,64,64]{1,3,2,0:T(8,128)} copy(f32[2,256,64,64]{3,2,1,0:T(8,128)} %reshape.150) | data formatting | bytes 16777216 | tf_op jit(solution)/shard_map/convert_element_type | solution.py:105
  173.1 1.8 fusion.21
  174.9 103.5 %all-gather.13.cloned.1.call-done = bf16[1024,256,64]{1,2,0:T(8,128)(2,1)} async-done(((bf16[64,256,64]{1,2,0:T(8,128)(2,1)}), bf16[1024,256,64]{1,2,0:T(8,128)(2,1)}) %all-gather.13.cloned.1.call-update) | async-done | bytes 33554448 | tf_op jit(solution)/shard_map/all_gather | solution.py:12
  278.5 238.5 %while.28 = (s32[]{:T(128)}, f32[64,256,64]{2,1,0:T(8,128)}, s32[]{:T(128)}, bf16[16,64]{1,0:T(8,128)(2,1)S(1)}, bf16[16,64,256,64]{2,3,1,0:T(8,128)(2,1)}, /*index=5*/s32[]{:T(128)}, s32[]{:T(128)}) while((s32[]{:T(128)}, f32[64,256,64]{2,1,0:T(8,128)}, s32[]{:T(128)}, bf16[16,64]{1,0:T(8,128)(2,1)S(1)}, ...), condition=%wide.region_7.8_spmd.clone, body=%wide.region_6.7_spmd.clone.sunk | while | flops 5242948 | bytes 18875112 | solution.py:29
  280.2 3.2 copy.102
  283.4 7.5 fusion.36
  292.7 3.2 copy.102
  295.8 10.0 %fusion.36 = f32[64,256,64]{2,1,0:T(8,128)} fusion(f32[64,256,64]{2,1,0:T(8,128)} %get-tuple-element.307, bf16[1,64,256,64]{3,2,1,0:T(8,128)(2,1)} %copy.102, f32[64]{0:T(128)S(1)} %exponential_bitcast_fusion.4, pred[]{:T(512)S(6)} %compare.7, pred[]{:T(512)S(6)} %lt.27), kind=kLoop, calls=%fused_computation.6.clone.1 | loop fusion | flops 5242880 | bytes 10486018 | tf_op jit(solution)/shard_map/while/body/eval_jaxpr/jit(_where)/select_n | solution.py:27
  307.6 3.2 copy.102
  310.8 10.8 %fusion.36 = f32[64,256,64]{2,1,0:T(8,128)} fusion(f32[64,256,64]{2,1,0:T(8,128)} %get-tuple-element.307, bf16[1,64,256,64]{3,2,1,0:T(8,128)(2,1)} %copy.102, f32[64]{0:T(128)S(1)} %exponential_bitcast_fusion.4, pred[]{:T(512)S(6)} %compare.7, pred[]{:T(512)S(6)} %lt.27), kind=kLoop, calls=%fused_computation.6.clone.1 | loop fusion | flops 5242880 | bytes 10486018 | tf_op jit(solution)/shard_map/while/body/eval_jaxpr/jit(_where)/select_n | solution.py:27
  323.3 3.2 copy.102
  326.5 9.9 %fusion.36 = f32[64,256,64]{2,1,0:T(8,128)} fusion(f32[64,256,64]{2,1,0:T(8,128)} %get-tuple-element.307, bf16[1,64,256,64]{3,2,1,0:T(8,128)(2,1)} %copy.102, f32[64]{0:T(128)S(1)} %exponential_bitcast_fusion.4, pred[]{:T(512)S(6)} %compare.7, pred[]{:T(512)S(6)} %lt.27), kind=kLoop, calls=%fused_computation.6.clone.1 | loop fusion | flops 5242880 | bytes 10486018 | tf_op jit(solution)/shard_map/while/body/eval_jaxpr/jit(_where)/select_n | solution.py:27
  336.4 2.0 constant_dynamic-slice_fusion.3
  338.4 3.2 copy.102
  341.6 10.2 %fusion.36 = f32[64,256,64]{2,1,0:T(8,128)} fusion(f32[64,256,64]{2,1,0:T(8,128)} %get-tuple-element.307, bf16[1,64,256,64]{3,2,1,0:T(8,128)(2,1)} %copy.102, f32[64]{0:T(128)S(1)} %exponential_bitcast_fusion.4, pred[]{:T(512)S(6)} %compare.7, pred[]{:T(512)S(6)} %lt.27), kind=kLoop, calls=%fused_computation.6.clone.1 | loop fusion | flops 5242880 | bytes 10486018 | tf_op jit(solution)/shard_map/while/body/eval_jaxpr/jit(_where)/select_n | solution.py:27
  353.5 3.2 copy.102
  356.7 9.9 %fusion.36 = f32[64,256,64]{2,1,0:T(8,128)} fusion(f32[64,256,64]{2,1,0:T(8,128)} %get-tuple-element.307, bf16[1,64,256,64]{3,2,1,0:T(8,128)(2,1)} %copy.102, f32[64]{0:T(128)S(1)} %exponential_bitcast_fusion.4, pred[]{:T(512)S(6)} %compare.7, pred[]{:T(512)S(6)} %lt.27), kind=kLoop, calls=%fused_computation.6.clone.1 | loop fusion | flops 5242880 | bytes 10486018 | tf_op jit(solution)/shard_map/while/body/eval_jaxpr/jit(_where)/select_n | solution.py:27
  368.4 3.2 copy.102
  371.5 10.0 %fusion.36 = f32[64,256,64]{2,1,0:T(8,128)} fusion(f32[64,256,64]{2,1,0:T(8,128)} %get-tuple-element.307, bf16[1,64,256,64]{3,2,1,0:T(8,128)(2,1)} %copy.102, f32[64]{0:T(128)S(1)} %exponential_bitcast_fusion.4, pred[]{:T(512)S(6)} %compare.7, pred[]{:T(512)S(6)} %lt.27), kind=kLoop, calls=%fused_computation.6.clone.1 | loop fusion | flops 5242880 | bytes 10486018 | tf_op jit(solution)/shard_map/while/body/eval_jaxpr/jit(_where)/select_n | solution.py:27
  383.2 3.2 copy.102
  386.4 10.5 %fusion.36 = f32[64,256,64]{2,1,0:T(8,128)} fusion(f32[64,256,64]{2,1,0:T(8,128)} %get-tuple-element.307, bf16[1,64,256,64]{3,2,1,0:T(8,128)(2,1)} %copy.102, f32[64]{0:T(128)S(1)} %exponential_bitcast_fusion.4, pred[]{:T(512)S(6)} %compare.7, pred[]{:T(512)S(6)} %lt.27), kind=kLoop, calls=%fused_computation.6.clone.1 | loop fusion | flops 5242880 | bytes 10486018 | tf_op jit(solution)/shard_map/while/body/eval_jaxpr/jit(_where)/select_n | solution.py:27
  398.7 3.2 copy.102
  401.8 10.4 %fusion.36 = f32[64,256,64]{2,1,0:T(8,128)} fusion(f32[64,256,64]{2,1,0:T(8,128)} %get-tuple-element.307, bf16[1,64,256,64]{3,2,1,0:T(8,128)(2,1)} %copy.102, f32[64]{0:T(128)S(1)} %exponential_bitcast_fusion.4, pred[]{:T(512)S(6)} %compare.7, pred[]{:T(512)S(6)} %lt.27), kind=kLoop, calls=%fused_computation.6.clone.1 | loop fusion | flops 5242880 | bytes 10486018 | tf_op jit(solution)/shard_map/while/body/eval_jaxpr/jit(_where)/select_n | solution.py:27
  414.0 3.2 copy.102
  417.2 10.1 %fusion.36 = f32[64,256,64]{2,1,0:T(8,128)} fusion(f32[64,256,64]{2,1,0:T(8,128)} %get-tuple-element.307, bf16[1,64,256,64]{3,2,1,0:T(8,128)(2,1)} %copy.102, f32[64]{0:T(128)S(1)} %exponential_bitcast_fusion.4, pred[]{:T(512)S(6)} %compare.7, pred[]{:T(512)S(6)} %lt.27), kind=kLoop, calls=%fused_computation.6.clone.1 | loop fusion | flops 5242880 | bytes 10486018 | tf_op jit(solution)/shard_map/while/body/eval_jaxpr/jit(_where)/select_n | solution.py:27
  429.0 3.2 copy.102
  432.2 10.6 %fusion.36 = f32[64,256,64]{2,1,0:T(8,128)} fusion(f32[64,256,64]{2,1,0:T(8,128)} %get-tuple-element.307, bf16[1,64,256,64]{3,2,1,0:T(8,128)(2,1)} %copy.102, f32[64]{0:T(128)S(1)} %exponential_bitcast_fusion.4, pred[]{:T(512)S(6)} %compare.7, pred[]{:T(512)S(6)} %lt.27), kind=kLoop, calls=%fused_computation.6.clone.1 | loop fusion | flops 5242880 | bytes 10486018 | tf_op jit(solution)/shard_map/while/body/eval_jaxpr/jit(_where)/select_n | solution.py:27
  444.5 3.2 copy.102
  447.7 9.9 %fusion.36 = f32[64,256,64]{2,1,0:T(8,128)} fusion(f32[64,256,64]{2,1,0:T(8,128)} %get-tuple-element.307, bf16[1,64,256,64]{3,2,1,0:T(8,128)(2,1)} %copy.102, f32[64]{0:T(128)S(1)} %exponential_bitcast_fusion.4, pred[]{:T(512)S(6)} %compare.7, pred[]{:T(512)S(6)} %lt.27), kind=kLoop, calls=%fused_computation.6.clone.1 | loop fusion | flops 5242880 | bytes 10486018 | tf_op jit(solution)/shard_map/while/body/eval_jaxpr/jit(_where)/select_n | solution.py:27
  459.4 3.2 copy.102
  462.5 9.9 %fusion.36 = f32[64,256,64]{2,1,0:T(8,128)} fusion(f32[64,256,64]{2,1,0:T(8,128)} %get-tuple-element.307, bf16[1,64,256,64]{3,2,1,0:T(8,128)(2,1)} %copy.102, f32[64]{0:T(128)S(1)} %exponential_bitcast_fusion.4, pred[]{:T(512)S(6)} %compare.7, pred[]{:T(512)S(6)} %lt.27), kind=kLoop, calls=%fused_computation.6.clone.1 | loop fusion | flops 5242880 | bytes 10486018 | tf_op jit(solution)/shard_map/while/body/eval_jaxpr/jit(_where)/select_n | solution.py:27
  474.2 3.2 copy.102
  477.4 9.9 %fusion.36 = f32[64,256,64]{2,1,0:T(8,128)} fusion(f32[64,256,64]{2,1,0:T(8,128)} %get-tuple-element.307, bf16[1,64,256,64]{3,2,1,0:T(8,128)(2,1)} %copy.102, f32[64]{0:T(128)S(1)} %exponential_bitcast_fusion.4, pred[]{:T(512)S(6)} %compare.7, pred[]{:T(512)S(6)} %lt.27), kind=kLoop, calls=%fused_computation.6.clone.1 | loop fusion | flops 5242880 | bytes 10486018 | tf_op jit(solution)/shard_map/while/body/eval_jaxpr/jit(_where)/select_n | solution.py:27
  489.0 3.2 copy.102
  492.2 9.9 %fusion.36 = f32[64,256,64]{2,1,0:T(8,128)} fusion(f32[64,256,64]{2,1,0:T(8,128)} %get-tuple-element.307, bf16[1,64,256,64]{3,2,1,0:T(8,128)(2,1)} %copy.102, f32[64]{0:T(128)S(1)} %exponential_bitcast_fusion.4, pred[]{:T(512)S(6)} %compare.7, pred[]{:T(512)S(6)} %lt.27), kind=kLoop, calls=%fused_computation.6.clone.1 | loop fusion | flops 5242880 | bytes 10486018 | tf_op jit(solution)/shard_map/while/body/eval_jaxpr/jit(_where)/select_n | solution.py:27
  503.8 3.2 copy.102
  507.0 9.9 %fusion.36 = f32[64,256,64]{2,1,0:T(8,128)} fusion(f32[64,256,64]{2,1,0:T(8,128)} %get-tuple-element.307, bf16[1,64,256,64]{3,2,1,0:T(8,128)(2,1)} %copy.102, f32[64]{0:T(128)S(1)} %exponential_bitcast_fusion.4, pred[]{:T(512)S(6)} %compare.7, pred[]{:T(512)S(6)} %lt.27), kind=kLoop, calls=%fused_computation.6.clone.1 | loop fusion | flops 5242880 | bytes 10486018 | tf_op jit(solution)/shard_map/while/body/eval_jaxpr/jit(_where)/select_n | solution.py:27
  516.9 5.9 broadcast_in_dim.54
  522.8 22.5 %fusion.4 = f32[2,64,64,256]{3,2,1,0:T(8,128)} fusion(bf16[2,256,64,256]{3,1,2,0:T(8,128)(2,1)} %bitcast.86, f32[2,64,256,64]{3,2,1,0:T(8,128)} %get-tuple-element.124, f32[64,256,64]{2,1,0:T(8,128)} %get-tuple-element.126, f32[2,64]{1,0:T(2,128)S(1)} %subtract_exponential_fusion), kind=kOutput, calls=%fused_computation.12 | convolution fusion | flops 6446645248 | bytes 37749248 | tf_op jit(solution)/shard_map/klhn,khnp->klhp/dot_general | solution.py:101
  545.4 11.7 %broadcast_in_dim.50 = f32[2,4,16,256,256]{4,3,2,1,0:T(8,128)} broadcast(f32[2,4,256,256]{3,2,1,0:T(8,128)S(1)} %copy-done.1), dimensions={0,1,3,4} | broadcast | bytes 35651584 | tf_op jit(solution)/shard_map/broadcast_in_dim | solution.py:66
  557.2 23.5 %multiply_reduce_fusion = (f32[2,256,64]{1,2,0:T(8,128)S(1)}, f32[2,256,64,64]{1,3,2,0:T(8,128)}) fusion(f32[2,256,64,64]{1,3,2,0:T(8,128)} %copy.75, bf16[2,256,64,64]{1,3,2,0:T(8,128)(2,1)S(1)} %copy-done, f32[64]{0:T(128)S(1)} %copy-done.12, f32[2,256,64]{1,2,0:T(8,128)S(1)} %copy-done.8, f32[2,64,64,256]{3,2,1,0:T(8,128)} %fusion.4, ...), kind=kOutput, calls=%fused_computation.25 | convolution fusion | flops 1140817920 | bytes 63373568 | tf_op jit(solution)/shard_map/khls,kshp->klhp/dot_general | solution.py:76
  580.6 14.4 %copy.76 = f32[2,256,64,64]{1,0,3,2:T(2,128)S(1)} copy(f32[2,256,64,64]{1,3,2,0:T(8,128)} %get-tuple-element.215) | data formatting | bytes 16777216 | tf_op jit(solution)/shard_map/mul | solution.py:104
  595.0 4.2 copy.88
  599.5 5.2 fusion.11
  604.7 23.8 %convolution_convert_fusion.1 = bf16[512,4096]{1,0:T(8,128)(2,1)} fusion(bf16[512,4096]{0,1:T(8,128)(2,1)} %fusion.11, bf16[4096,4096]{1,0:T(8,128)(2,1)} %all-gather.7.cloned.1.call-done), kind=kOutput, calls=%fused_computation.29 | convolution fusion | flops 17181966336 | bytes 41943040 | tf_op jit(solution)/shard_map/dot_general | solution.py:110
  630.8 54.2 %reduce-scatter.2.cloned.1.call-done = bf16[256,4096]{1,0:T(8,128)(2,1)} async-done(((bf16[512,4096]{1,0:T(8,128)(2,1)}), bf16[256,4096]{1,0:T(8,128)(2,1)}) %reduce-scatter.2.cloned.1.call-update) | async-done | bytes 2097168 | tf_op jit(solution)/shard_map/reduce_scatter | solution.py:115
  685.0 5.1 fusion.20
  690.1 2.9 fusion.17
  694.3 1.9 fusion.19
  696.3 158.4 %all-gather.11.cloned.1.call-done = bf16[4096,4096]{1,0:T(8,128)(2,1)} async-done(((bf16[256,4096]{1,0:T(8,128)(2,1)}), bf16[4096,4096]{1,0:T(8,128)(2,1)}) %all-gather.11.cloned.1.call-update) | async-done | bytes 33554448 | tf_op jit(solution)/shard_map/all_gather | solution.py:131
  854.7 58.8 %all-gather.9.cloned.1.call-done = bf16[512,4096]{1,0:T(8,128)(2,1)} async-done(((bf16[256,4096]{1,0:T(8,128)(2,1)}), bf16[512,4096]{1,0:T(8,128)(2,1)}) %all-gather.9.cloned.1.call-update) | async-done | bytes 4194320 | tf_op jit(solution)/shard_map/all_gather | solution.py:128
  913.5 23.6 %convolution_convert_fusion = bf16[512,4096]{1,0:T(8,128)(2,1)} fusion(bf16[512,4096]{1,0:T(8,128)(2,1)} %all-gather.9.cloned.1.call-done, bf16[4096,4096]{1,0:T(8,128)(2,1)} %all-gather.11.cloned.1.call-done), kind=kOutput, calls=%fused_computation.28 | convolution fusion | flops 17181966336 | bytes 41943040 | tf_op jit(solution)/shard_map/dot_general | solution.py:129
  (99 shorter events, 36.2 us)
Async XLA Ops:
  7.2 271.3 %all-gather.13.cloned.1.call-start = ((), (), s32[]{:S(2)}) async-start(), calls=%async_computation.5 | async-start | bytes 35651584 | tf_op jit(solution)/shard_map/all_gather | solution.py:12
  9.7 1.0 copy-start.6
  101.4 6.7 copy-start.13
  101.4 44.2 %copy-start.5 = (bf16[512,4,256]{2,1,0:T(4,128)(2,1)S(1)}, bf16[512,4,256]{2,1,0:T(4,128)(2,1)}, u32[]{:S(2)}) copy-start(bf16[512,4,256]{2,1,0:T(4,128)(2,1)} %param.19) | copy-start | bytes 3145732
  107.3 497.5 %all-gather.7.cloned.1.call-start = ((), (), s32[]{:S(2)}) async-start(), calls=%async_computation.1 | async-start | bytes 35651584 | tf_op jit(solution)/shard_map/all_gather | solution.py:112
  108.0 577.0 %reduce-scatter.2.cloned.1.call-start = ((), (), s32[]{:S(2)}) async-start(), calls=%async_computation.2 | async-start | bytes 6291456 | tf_op jit(solution)/shard_map/reduce_scatter | solution.py:115
  158.5 14.6 %copy-start.4 = (bf16[512,4,256]{2,1,0:T(4,128)(2,1)S(1)}, bf16[512,4,256]{2,1,0:T(4,128)(2,1)}, u32[]{:S(2)}) copy-start(bf16[512,4,256]{2,1,0:T(4,128)(2,1)} %param.18) | copy-start | bytes 3145732
  522.8 22.6 %copy-start.1 = (f32[2,4,256,256]{3,2,1,0:T(8,128)S(1)}, f32[2,4,256,256]{3,2,1,0:T(8,128)}, u32[]{:S(2)}) copy-start(f32[2,4,256,256]{3,2,1,0:T(8,128)} %fusion.21) | copy-start | bytes 6291460
  545.4 11.8 %copy-start = (bf16[2,256,64,64]{1,3,2,0:T(8,128)(2,1)S(1)}, bf16[2,256,64,64]{1,3,2,0:T(8,128)(2,1)}, u32[]{:S(2)}) copy-start(bf16[2,256,64,64]{1,3,2,0:T(8,128)(2,1)} %copy.64) | copy-start | bytes 12582916
  545.4 11.8 %copy-start.7 = (f32[2,64,256]{2,1,0:T(8,128)S(1)}, f32[2,64,256]{2,1,0:T(8,128)}, u32[]{:S(2)}) copy-start(f32[2,64,256]{2,1,0:T(8,128)} %copy-done.6) | copy-start | bytes 393220
  545.4 11.8 %copy-start.8 = (f32[2,256,64]{1,2,0:T(8,128)S(1)}, f32[2,256,64]{1,2,0:T(8,128)}, u32[]{:S(2)}) copy-start(f32[2,256,64]{1,2,0:T(8,128)} %get-tuple-element.212) | copy-start | bytes 393220
  545.4 11.8 %copy-start.12 = (f32[64]{0:T(128)S(1)}, f32[64]{0:T(128)}, u32[]{:S(2)}) copy-start(f32[64]{0:T(128)} %param.21) | copy-start | bytes 772
  595.0 4.5 copy-start.10
  604.7 24.7 %copy-start.9 = (f32[4096]{0:T(1024)S(1)}, f32[4096]{0:T(1024)}, u32[]{:S(2)}) copy-start(f32[4096]{0:T(1024)} %param.25) | copy-start | bytes 49156
  604.7 80.3 %copy-start.2 = (bf16[256,4096]{1,0:T(8,128)(2,1)S(1)}, bf16[256,4096]{1,0:T(8,128)(2,1)}, u32[]{:S(2)}) copy-start(bf16[256,4096]{1,0:T(8,128)(2,1)} %param.24) | copy-start | bytes 6291460
  628.6 65.8 %copy-start.11 = (f32[4096]{0:T(1024)S(1)}, f32[4096]{0:T(1024)}, u32[]{:S(2)}) copy-start(f32[4096]{0:T(1024)} %param.26) | copy-start | bytes 49156
  628.6 226.1 %all-gather.11.cloned.1.call-start = ((), (), s32[]{:S(2)}) async-start(), calls=%async_computation.4 | async-start | bytes 35651584 | tf_op jit(solution)/shard_map/all_gather | solution.py:131
  629.2 284.3 %all-gather.9.cloned.1.call-start = ((), (), s32[]{:S(2)}) async-start(), calls=%async_computation.3 | async-start | bytes 6291456 | tf_op jit(solution)/shard_map/all_gather | solution.py:128
  693.0 1.3 copy-start.3
Sparse Core Ops, SparseCore 0:
  107.4 171.0 all-gather.12
  280.0 177.3 all-gather.6
  628.7 56.2 reduce-scatter.1
  686.6 168.0 all-gather.10
  856.7 56.7 all-gather.8
where the time goes:
time: 953 us; the launch traced here: 944 us
  waiting for transfers between devices  376 us (39%)
  other arithmetic  206 us (22%)
  local copies, waits for them, and re-layouts  187 us (20%)
  matrix products  122 us (13%)
  blocking collectives  36 us (4%)
  between operations  15.7 us (2%)
    select_n x16, other arithmetic, turn(): return jax.tree.map(lambda a, b: jnp.where(reached, a, b), new, before)  160 us
    all_gather x1, waiting for transfers between devices, body(): lax.all_gather(w_in, 'seq', axis=0, tiled=True)  158 us
    all_gather x1, waiting for transfers between devices, prefix(): lax.all_gather(part.astype(kind), axis)  104 us
    dynamic_slice x32, local copies, waits for them, and re-layouts, turn(): part[k].astype(own.dtype)  78.7 us
    all_gather x1, waiting for transfers between devices, body(): all_rows = lax.all_gather(normed, 'head', axis=0, tiled=True)  58.8 us
    reduce_scatter x1, waiting for transfers between devices, body(): lax.psum_scatter(partial_sum.astype(jnp.bfloat16), 'head', scatter_dimens...  54.2 us
    unnamed x1, blocking collectives  36 us
    convert_element_type x2, local copies, waits for them, and re-layouts, body(): gate_z.reshape(block_count, SPAN, head_count, head_width)  27.2 us
  transfers between devices with their start and end apart: 5, of which 4 were waited for; matrix products, arithmetic and copies ran while one was open for 39% of the time, Pallas kernels for 0%

commit v1 on v0

v1 whole, which is shorter than its diff:
```python
import functools

import jax
import jax.numpy as jnp
from jax import lax
from jax.experimental import pallas as pl
from jax.experimental.pallas import tpu as pltpu
from jax.sharding import PartitionSpec as P

SPAN = 256
EXTRA = 16
VMEM_LIMIT = 48 * 1024 * 1024
IN_CHUNKS = 2


def expand(values, width):
    heads = values.shape[1]
    shape = (heads, heads * width)
    spread = lax.broadcasted_iota(jnp.int32, shape, 1) // width
    spread = (spread == lax.broadcasted_iota(jnp.int32, shape, 0)).astype(jnp.bfloat16)
    high = values.astype(jnp.bfloat16)
    low = (values - high.astype(jnp.float32)).astype(jnp.bfloat16)
    return jnp.dot(high, spread, preferred_element_type=jnp.float32) + jnp.dot(
        low, spread, preferred_element_type=jnp.float32
    )


def state_kernel(blocks, width, x_ref, b_ref, cum_ref, sent_ref, local_ref):
    state_width = b_ref.shape[1]
    slices, _, lanes = sent_ref.shape
    state = None
    total = None
    for k in range(blocks):
        rows = pl.ds(k * SPAN, SPAN)
        cum = cum_ref[0, rows, :]
        last = cum[SPAN - 1 : SPAN, :]
        scale = expand(jnp.exp(last - cum), width)
        weighted = (x_ref[rows, :].astype(jnp.float32) * scale).astype(jnp.bfloat16)
        new = lax.dot_general(
            b_ref[rows, :], weighted, (((0,), (0,)), ((), ())), preferred_element_type=jnp.float32
        )
        if state is None:
            state, total = new, last
        else:
            decay = expand(jnp.exp(jnp.broadcast_to(last, (EXTRA, last.shape[1]))), width)
            state = decay[0:1, :] * state + new
            total = total + last
        if k < blocks - 1:
            local_ref[k, :, :] = state.astype(jnp.bfloat16)
    if blocks == 1:
        local_ref[0, :, :] = jnp.zeros_like(local_ref[0])
    whole = expand(jnp.exp(jnp.broadcast_to(total, (EXTRA, total.shape[1]))), width)
    high = whole.astype(jnp.bfloat16).astype(jnp.float32)
    row = lax.broadcasted_iota(jnp.int32, whole.shape, 0)
    marks = jnp.where(row == 0, high, jnp.where(row == 1, whole - high, 0.0)).astype(jnp.bfloat16)
    state = state.astype(jnp.bfloat16)
    for i in range(slices):
        sent_ref[i, 0:state_width, :] = state[:, i * lanes : (i + 1) * lanes]
        sent_ref[i, state_width : state_width + EXTRA, :] = marks[:, i * lanes : (i + 1) * lanes]


def scan_kernel(sent_ref, out_ref):
    devices, state_width, lanes = out_ref.shape
    carry = jnp.zeros((state_width, lanes), jnp.float32)
    for k in range(devices):
        out_ref[k, :, :] = carry.astype(jnp.bfloat16)
        marks = sent_ref[k, state_width : state_width + EXTRA, :].astype(jnp.float32)
        decay = marks[0:1, :] + marks[1:2, :]
        carry = decay * carry + sent_ref[k, 0:state_width, :].astype(jnp.float32)


def output_kernel(
    blocks, width, x_ref, z_ref, b_ref, c_ref, cum_ref, cum_t_ref, skip_ref, gain_ref, in_ref,
    local_ref, out_ref,
):
    per_group = cum_ref.shape[2]
    slices = in_ref.shape[0]
    incoming = jnp.concatenate([in_ref[i] for i in range(slices)], axis=1).astype(jnp.float32)
    causal = lax.broadcasted_iota(jnp.int32, (SPAN, SPAN), 0) >= lax.broadcasted_iota(
        jnp.int32, (SPAN, SPAN), 1
    )
    first = lax.broadcasted_iota(jnp.int32, (SPAN, 2 * width), 1) < width
    before = None
    for k in range(blocks):
        rows = pl.ds(k * SPAN, SPAN)
        c_block = c_ref[rows, :]
        scores = lax.dot_general(
            c_block, b_ref[rows, :], (((1,), (1,)), ((), ())), preferred_element_type=jnp.float32
        )
        scores = jnp.where(causal, scores, 0.0)
        cum = cum_ref[0, rows, :]
        grown = expand(jnp.exp(cum), width)
        if k == 0:
            start = incoming
        else:
            decay = expand(jnp.exp(jnp.broadcast_to(before, (EXTRA, per_group))), width)
            start = decay[0:1, :] * incoming + local_ref[k - 1].astype(jnp.float32)
        last = cum[SPAN - 1 : SPAN, :]
        before = last if before is None else before + last
        carried = jnp.dot(c_block, start.astype(jnp.bfloat16), preferred_element_type=jnp.float32)
        x_block = x_ref[rows, :]
        pieces = []
        for pair in range(per_group // 2):
            x_pair = x_block[:, pair * 2 * width : (pair + 1) * 2 * width]
            both = []
            for head in (2 * pair, 2 * pair + 1):
                gap = cum[:, head : head + 1] - cum_t_ref[0, head : head + 1, rows]
                mixing = (jnp.exp(jnp.minimum(gap, 0.0)) * scores).astype(jnp.bfloat16)
                both.append(jnp.dot(mixing, x_pair, preferred_element_type=jnp.float32))
            pieces.append(jnp.where(first, both[0], both[1]))
        mixed = jnp.concatenate(pieces, axis=1) + carried * grown
        mixed = mixed + skip_ref[...] * x_block.astype(jnp.float32)
        z = z_ref[rows, :].astype(jnp.float32)
        gated = mixed * (z / (1.0 + jnp.exp(-z)))
        mean = jnp.mean(gated * gated, axis=-1, keepdims=True)
        out_ref[rows, :] = (gated * lax.rsqrt(mean + 1e-05) * gain_ref[...]).astype(jnp.bfloat16)


def mixer(xin, gate_z, b_proj, c_proj, log_retain, skip_d, norm_gain, devices):
    seq_rows, channels = xin.shape
    heads = log_retain.shape[1]
    width = channels // heads
    _, groups, state_width = b_proj.shape
    per_group = heads // groups
    group_lanes = channels // groups
    blocks = seq_rows // SPAN
    lanes = channels // devices
    slices = devices // groups
    tri = jnp.tril(jnp.ones((SPAN, SPAN), jnp.float32))
    cum = jnp.einsum(
        "ts,ksh->kth",
        tri,
        log_retain.reshape(blocks, SPAN, heads),
        precision=lax.Precision.HIGHEST,
    ).reshape(seq_rows, groups, per_group)
    cum_g = jnp.transpose(cum, (1, 0, 2))
    cum_t = jnp.transpose(cum, (1, 2, 0))
    b_flat = b_proj.reshape(seq_rows, groups * state_width)
    c_flat = c_proj.reshape(seq_rows, groups * state_width)
    params = pltpu.CompilerParams(vmem_limit_bytes=VMEM_LIMIT)
    wide = pl.BlockSpec((seq_rows, group_lanes), lambda g: (0, g))
    proj = pl.BlockSpec((seq_rows, state_width), lambda g: (0, g))
    cum_spec = pl.BlockSpec((1, seq_rows, per_group), lambda g: (g, 0, 0))
    local_count = max(blocks - 1, 1)
    local_spec = pl.BlockSpec((local_count, state_width, group_lanes), lambda g: (0, 0, g))
    sent, local = pl.pallas_call(
        functools.partial(state_kernel, blocks, width),
        grid=(groups,),
        in_specs=[wide, proj, cum_spec],
        out_specs=[
            pl.BlockSpec((slices, state_width + EXTRA, lanes), lambda g: (g, 0, 0)),
            local_spec,
        ],
        out_shape=[
            jax.ShapeDtypeStruct((devices, state_width + EXTRA, lanes), jnp.bfloat16),
            jax.ShapeDtypeStruct((local_count, state_width, channels), jnp.bfloat16),
        ],
        compiler_params=params,
        name="block_states",
    )(xin, b_flat, cum_g)
    gathered = lax.all_to_all(sent, "seq", 0, 0, tiled=True)
    starts = pl.pallas_call(
        scan_kernel,
        in_specs=[pl.BlockSpec(memory_space=pltpu.VMEM)],
        out_specs=pl.BlockSpec(memory_space=pltpu.VMEM),
        out_shape=jax.ShapeDtypeStruct((devices, state_width, lanes), jnp.bfloat16),
        compiler_params=params,
        name="state_scan",
    )(gathered)
    incoming = lax.all_to_all(starts, "seq", 0, 0, tiled=True)
    row_spec = pl.BlockSpec((1, group_lanes), lambda g: (0, g))
    return pl.pallas_call(
        functools.partial(output_kernel, blocks, width),
        grid=(groups,),
        in_specs=[
            wide,
            wide,
            proj,
            proj,
            cum_spec,
            pl.BlockSpec((1, per_group, seq_rows), lambda g: (g, 0, 0)),
            row_spec,
            row_spec,
            pl.BlockSpec((slices, state_width, lanes), lambda g: (g, 0, 0)),
            local_spec,
        ],
        out_specs=wide,
        out_shape=jax.ShapeDtypeStruct((seq_rows, channels), jnp.bfloat16),
        compiler_params=params,
        name="mixer_out",
    )(
        xin,
        gate_z,
        b_flat,
        c_flat,
        cum_g,
        cum_t,
        jnp.repeat(skip_d, width)[None, :],
        norm_gain[None, :],
        incoming,
        local,
    )


def body(
    xin,
    gate_z,
    b_proj,
    c_proj,
    log_retain,
    skip_d,
    norm_gain,
    w_out,
    residual,
    refusal,
    stream_gain,
    w_in,
):
    devices = lax.axis_size("seq")
    head_devices = lax.axis_size("head")
    place = lax.axis_index("head")
    seq_rows, channels = xin.shape
    own_rows = seq_rows // head_devices

    def shift(array, by):
        pairs = [(i, (i + by) % head_devices) for i in range(head_devices)]
        return lax.ppermute(array, "head", pairs)

    w_out_all = lax.all_gather(w_out, "seq", axis=1, tiled=True)
    in_lanes = w_in.shape[1] // IN_CHUNKS
    w_in_all = [
        lax.all_gather(w_in[:, i * in_lanes : (i + 1) * in_lanes], "seq", axis=0, tiled=True)
        for i in range(IN_CHUNKS)
    ]
    ssd_out = mixer(xin, gate_z, b_proj, c_proj, log_retain, skip_d, norm_gain, devices)

    def partial_of(index):
        rows = lax.dynamic_slice_in_dim(ssd_out, index * own_rows, own_rows, 0)
        return jnp.dot(rows, w_out_all, preferred_element_type=jnp.float32).astype(jnp.bfloat16)

    arrived = [
        shift(partial_of(lax.rem(place + by, head_devices)), by) for by in range(1, head_devices)
    ]
    mixer_out = partial_of(place).astype(jnp.float32)
    for part in arrived:
        mixer_out = mixer_out + part.astype(jnp.float32)
    unit = refusal / jnp.sqrt(jnp.sum(refusal * refusal) + 1e-06)
    hidden = residual.astype(jnp.float32) + mixer_out
    coef = jnp.sum(hidden * unit[None, :], axis=-1, keepdims=True)
    stream = (hidden - coef * unit[None, :]).astype(jnp.bfloat16)
    stream_float = stream.astype(jnp.float32)
    normed = (
        stream_float
        * lax.rsqrt(jnp.mean(stream_float * stream_float, axis=-1, keepdims=True) + 1e-05)
        * stream_gain[None, :]
    ).astype(jnp.bfloat16)
    all_rows = jnp.zeros((seq_rows, normed.shape[1]), jnp.bfloat16)
    for by in range(head_devices):
        rows = normed if by == 0 else shift(normed, by)
        source = lax.rem(place - by + head_devices, head_devices)
        all_rows = lax.dynamic_update_slice_in_dim(all_rows, rows, source * own_rows, 0)
    next_x = jnp.concatenate(
        [
            jnp.dot(all_rows, weight, preferred_element_type=jnp.float32).astype(jnp.bfloat16)
            for weight in w_in_all
        ],
        axis=1,
    )
    return (stream, next_x)


def solution(mesh):
    in_specs = (
        P("seq", "head"),
        P("seq", "head"),
        P("seq", "head", None),
        P("seq", "head", None),
        P("seq", "head"),
        P("head"),
        P("head"),
        P("head", "seq"),
        P(("seq", "head"), None),
        P(),
        P(),
        P("seq", "head"),
    )
    out_specs = (P(("seq", "head"), None), P("seq", "head"))
    return jax.shard_map(body, mesh=mesh, in_specs=in_specs, out_specs=out_specs, check_vma=False)
```

time: 953 us -> 558 us (0.59)
  other arithmetic: 206 us -> 5.96 us
  local copies, waits for them, and re-layouts: 187 us -> 12.5 us
  matrix products: 122 us -> 62.9 us
  blocking collectives: 36 us -> 82.9 us
  waiting for transfers between devices: 376 us -> 345 us
  Pallas kernels: 0 us -> 26.3 us
    select_n x16 -> x0, other arithmetic: 160 us -> none  [turn(): return jax.tree.map(lambda a, b: jnp.where(reached, a, b), new, before)]
    all_gather x4 -> x3, waiting for transfers between devices: 321 us -> 200 us  [the longest x2 104 us: body(): lax.all_gather(w_in[:, i * in_lanes:(i + 1) * in_lanes], 'seq', axis=0, t...]
    ppermute x0 -> x2, waiting for transfers between devices: none -> 91 us  [shift(): return lax.ppermute(array, 'head', pairs)]
    all_to_all x0 -> x1, blocking collectives: none -> 82.9 us  [mixer(): gathered = lax.all_to_all(sent, 'seq', 0, 0, tiled=True)]
    dynamic_slice x32 -> x0, local copies, waits for them, and re-layouts: 78.7 us -> none  [turn(): part[k].astype(own.dtype)]
    dot_general x7 -> x4, matrix products: 122 us -> 62.5 us  [the longest x2 35 us: partial_of(): jnp.dot(rows, w_out_all, preferred_element_type=jnp.float32)]
    reduce_scatter x1 -> x0, waiting for transfers between devices: 54.2 us -> none  [body(): lax.psum_scatter(partial_sum.astype(jnp.bfloat16), 'head', scatter_dimens...]
    all_to_all x0 -> x1, waiting for transfers between devices: none -> 51.9 us  [mixer(): incoming = lax.all_to_all(starts, 'seq', 0, 0, tiled=True)]
  transfers between devices with their start and end apart: 5 -> 6, of which waited for: 4 -> 5; matrix products, arithmetic and copies ran while one was open for 39% -> 11% of each run, Pallas kernels for 0% -> 5%
where the time goes in v1:
time: 558 us; the launch traced here: 557 us
  waiting for transfers between devices  345 us (62%)
  blocking collectives  82.9 us (15%)
  matrix products  62.9 us (11%)
  Pallas kernels  26.3 us (5%)
  between operations  14.6 us (3%)
  local copies, waits for them, and re-layouts  12.5 us (2%)
  starting transfers between devices  7.65 us (1%)
  other arithmetic  5.96 us (1%)
    all_gather x2, waiting for transfers between devices, body(): lax.all_gather(w_in[:, i * in_lanes:(i + 1) * in_lanes], 'seq', axis=0, t...  104 us
    all_gather x1, waiting for transfers between devices, body(): w_out_all = lax.all_gather(w_out, 'seq', axis=1, tiled=True)  96.2 us
    ppermute x2, waiting for transfers between devices, shift(): return lax.ppermute(array, 'head', pairs)  91 us
    all_to_all x1, blocking collectives, mixer(): gathered = lax.all_to_all(sent, 'seq', 0, 0, tiled=True)  82.9 us
    all_to_all x1, waiting for transfers between devices, mixer(): incoming = lax.all_to_all(starts, 'seq', 0, 0, tiled=True)  51.9 us
    dot_general x2, matrix products, partial_of(): jnp.dot(rows, w_out_all, preferred_element_type=jnp.float32)  35 us
    dot_general x2, matrix products, body(): jnp.dot(all_rows, weight, preferred_element_type=jnp.float32)  27.5 us
    pallas_call x1, Pallas kernels, mixer(): pl.pallas_call(functools.partial(output_kernel, blocks, width), grid=(gro...  18.1 us
  transfers between devices with their start and end apart: 6, of which 5 were waited for; matrix products, arithmetic and copies ran while one was open for 11% of the time, Pallas kernels for 5%

profile of v1, /device:TPU:0, one launch (start us, length us, event | category | flops | bytes accessed | tf_op | source)
XLA Modules:
  0.0 557.4 jit_solution(9878925014799895361)
XLA Ops:
  7.2 0.0 copy-start.5
  7.2 0.0 all-gather.4.cloned.1.call-start
  7.2 0.7 all-gather.4.cloned.1.call-update
  7.9 0.0 copy-start.4
  7.9 0.0 all-gather.8.cloned.1.call-start
  8.0 3.2 fusion.17
  11.2 0.0 all-gather.8.cloned.1.call-update
  11.2 0.0 all-gather.6.cloned.1.call-start
  11.2 0.7 all-gather.6.cloned.1.call-update
  11.9 0.0 copy-done.5
  12.0 0.4 fusion.8
  12.4 0.1 copy.15
  12.5 0.1 reshape.30
  12.6 0.3 copy.17.cum_ref
  12.9 0.0 copy-done.4
  13.0 0.2 copy.19
  13.2 7.7 %block_states.1 = (bf16[16,272,256]{2,1,0:T(8,128)(2,1)}, bf16[1,256,4096]{2,1,0:T(8,128)(2,1)S(1)}) custom-call(bf16[512,4096]{1,0:T(8,128)(2,1)} %x_ref.3, bf16[512,1024]{1,0:T(8,128)(2,1)S(1)} %bitcast.26, f32[4,512,16]{2,1,0:T(8,128)S(1)} %copy.17.cum_ref), custom_call_target="tpu_custom_call" | custom-call | tf_op jit(solution)/shard_map/block_states/pallas_call | solution.py:146
  20.9 0.0 copy-start.1
  20.9 1.4 copy-done.1
  22.3 82.9 %all_to_all.10.sent_ref = bf16[16,272,256]{2,1,0:T(8,128)(2,1)S(1)} all-to-all(bf16[16,272,256]{2,1,0:T(8,128)(2,1)} %get-tuple-element.4), channel_id=1, replica_groups=mesh['seq'=16,'head'=2] {'seq'}, dimensions={0} | all-to-all | bytes 4456448 | tf_op jit(solution)/shard_map/all_to_all | solution.py:161
  105.2 0.5 state_scan.1
  105.6 0.0 copy-start
  105.7 1.3 copy-done
  107.0 0.0 copy-start.8
  107.0 0.0 copy-start.2
  107.0 4.8 all-to-all-start.1
  111.7 1.5 copy.20
  113.2 0.0 copy-done.8
  113.2 0.1 broadcast_in_dim.23
  113.3 0.1 broadcast_in_dim_reshape.3.skip_ref
  113.4 51.9 %all-to-all-done.1.in_ref = bf16[16,256,256]{2,1,0:T(8,128)(2,1)} async-done(((bf16[16,256,256]{2,1,0:T(8,128)(2,1)}), bf16[16,256,256]{2,1,0:T(8,128)(2,1)}, u32[]{:S(2)}, u32[]{:S(2)}) %all-to-all-start.1) | async-done | bytes 2097184 | tf_op jit(solution)/shard_map/all_to_all | solution.py:170
  165.3 0.0 copy-done.2
  165.3 18.1 %mixer_out.1 = bf16[512,4096]{1,0:T(8,128)(2,1)} custom-call(bf16[512,4096]{1,0:T(8,128)(2,1)} %x_ref.3, bf16[512,4096]{1,0:T(8,128)(2,1)} %z_ref.1, bf16[512,1024]{1,0:T(8,128)(2,1)S(1)} %bitcast.27, bf16[512,1024]{1,0:T(8,128)(2,1)S(1)} %bitcast.28, f32[4,512,16]{2,1,0:T(8,128)S(1)} %copy.17.cum_ref, f32[4,16,512]{2,1,0:T(8,128)S(1)} %bitcast.30, ...), custom_call_target="tpu_custom_call" | custom-call | tf_op jit(solution)/shard_map/mixer_out/pallas_call | solution.py:172
  183.4 0.0 copy-start.6
  183.4 0.0 copy-start.9
  183.4 96.2 %all-gather.4.cloned.1.call-done = bf16[4096,4096]{1,0:T(8,128)(2,1)} async-done(((bf16[4096,256]{1,0:T(8,128)(2,1)}), bf16[4096,4096]{1,0:T(8,128)(2,1)}) %all-gather.4.cloned.1.call-update) | async-done | bytes 33554448 | tf_op jit(solution)/shard_map/all_gather | solution.py:229
  279.7 18.0 %convolution_convert_fusion = bf16[256,4096]{1,0:T(8,128)(2,1)} fusion(bf16[4096,4096]{1,0:T(8,128)(2,1)} %all-gather.4.cloned.1.call-done, bf16[512,4096]{1,0:T(8,128)(2,1)} %mixer_out.1, s32[]{:T(128)S(6)} %select_n.16), kind=kOutput, calls=%fused_computation.2 | convolution fusion | flops 8590983168 | bytes 37748740 | tf_op jit(solution)/shard_map/dot_general | solution.py:239
  297.7 1.4 collective-permute-start
  299.1 0.0 copy-done.6
  299.1 0.6 multiply_reduce_fusion.1
  300.3 45.5 %collective-permute-done = bf16[256,4096]{1,0:T(8,128)(2,1)} collective-permute-done((bf16[256,4096]{1,0:T(8,128)(2,1)}, bf16[256,4096]{1,0:T(8,128)(2,1)}, u32[]{:S(2)}, u32[]{:S(2)}) %collective-permute-start) | collective-permute-done | bytes 2097184 | tf_op jit(solution)/shard_map/ppermute | solution.py:227
  345.8 0.0 copy-done.9
  345.8 16.9 %multiply_reduce_fusion = (f32[256]{0:T(256)S(1)}, f32[256,4096]{1,0:T(8,128)S(1)}) fusion(f32[4096]{0:T(1024)S(1)} %broadcast_divide_fusion, bf16[256,4096]{1,0:T(8,128)(2,1)} %collective-permute-done, bf16[4096,4096]{1,0:T(8,128)(2,1)} %all-gather.4.cloned.1.call-done, bf16[512,4096]{1,0:T(8,128)(2,1)} %mixer_out.1, s32[]{:T(128)S(6)} %select_n.15, ...), kind=kOutput, calls=%fused_computation.10 | convolution fusion | flops 8598323200 | bytes 44057604 | tf_op jit(solution)/shard_map/dot_general | solution.py:239
  362.7 0.0 copy-start.7
  362.7 0.8 fusion.1
  363.5 0.0 copy-start.3
  363.5 2.7 broadcast_in_dim.25
  366.2 0.0 copy-done.7
  366.2 2.2 constant_dynamic-update-slice_fusion.1
  368.4 0.0 copy-done.3
  368.4 1.4 collective-permute-start.1
  369.8 45.6 %collective-permute-done.1 = bf16[256,4096]{1,0:T(8,128)(2,1)S(1)} collective-permute-done((bf16[256,4096]{1,0:T(8,128)(2,1)S(1)}, bf16[256,4096]{1,0:T(8,128)(2,1)S(1)}, u32[]{:S(2)}, u32[]{:S(2)}) %collective-permute-start.1) | collective-permute-done | bytes 2097184 | tf_op jit(solution)/shard_map/ppermute | solution.py:227
  415.3 1.5 constant_dynamic-update-slice_fusion
  416.8 0.0 all-gather.8.cloned.1.call-done
  416.8 13.9 %convolution_convert_fusion.2 = bf16[512,2048]{1,0:T(8,128)(2,1)S(1)} fusion(bf16[512,4096]{1,0:T(8,128)(2,1)} %constant_dynamic-update-slice_fusion, bf16[4096,2048]{1,0:T(8,128)(2,1)} %all-gather.8.cloned.1.call-done), kind=kOutput, calls=%fused_computation.12 | convolution fusion | flops 8590983168 | bytes 23068672 | tf_op jit(solution)/shard_map/dot_general | solution.py:264
  430.7 104.1 %all-gather.6.cloned.1.call-done = bf16[4096,2048]{1,0:T(8,128)(2,1)} async-done(((bf16[256,2048]{1,0:T(8,128)(2,1)}), bf16[4096,2048]{1,0:T(8,128)(2,1)}) %all-gather.6.cloned.1.call-update) | async-done | bytes 16777232 | tf_op jit(solution)/shard_map/all_gather | solution.py:232
  534.9 13.6 %convolution_convert_fusion.3 = bf16[512,2048]{1,0:T(8,128)(2,1)S(1)} fusion(bf16[512,4096]{1,0:T(8,128)(2,1)} %constant_dynamic-update-slice_fusion, bf16[4096,2048]{1,0:T(8,128)(2,1)} %all-gather.6.cloned.1.call-done), kind=kOutput, calls=%fused_computation.13 | convolution fusion | flops 8590983168 | bytes 23068672 | tf_op jit(solution)/shard_map/dot_general | solution.py:264
  548.5 2.4 pad_maximum_fusion
  (3 shorter events, 0.0 us)
Async XLA Ops:
  7.2 4.8 copy-start.5
  7.2 272.5 %all-gather.4.cloned.1.call-start = ((), (), s32[]{:S(2)}) async-start(), calls=%async_computation.2 | async-start | bytes 35651584 | tf_op jit(solution)/shard_map/all_gather | solution.py:229
  7.9 5.0 copy-start.4
  7.9 408.9 %all-gather.8.cloned.1.call-start = ((), (), s32[]{:S(2)}) async-start(), calls=%async_computation.4 | async-start | bytes 17825792 | tf_op jit(solution)/shard_map/all_gather | solution.py:232
  11.2 523.7 %all-gather.6.cloned.1.call-start = ((), (), s32[]{:S(2)}) async-start(), calls=%async_computation.3 | async-start | bytes 17825792 | tf_op jit(solution)/shard_map/all_gather | solution.py:232
  20.9 1.4 copy-start.1
  105.6 1.3 copy-start
  107.0 6.3 %copy-start.8 = (f32[64]{0:T(128)S(1)}, f32[64]{0:T(128)}, u32[]{:S(2)}) copy-start(f32[64]{0:T(128)} %param.17) | copy-start | bytes 772
  107.0 58.4 %copy-start.2 = (f32[4096]{0:T(1024)S(1)}, f32[4096]{0:T(1024)}, u32[]{:S(2)}) copy-start(f32[4096]{0:T(1024)} %param.18) | copy-start | bytes 49156
  107.0 58.4 %all-to-all-start.1 = ((bf16[16,256,256]{2,1,0:T(8,128)(2,1)}), bf16[16,256,256]{2,1,0:T(8,128)(2,1)}, u32[]{:S(2)}, u32[]{:S(2)}) async-start(bf16[16,256,256]{2,1,0:T(8,128)(2,1)} %copy-done), calls=%async_computation.1 | async-start | bytes 4194304 | tf_op jit(solution)/shard_map/all_to_all | solution.py:170
  183.4 115.6 %copy-start.6 = (f32[4096]{0:T(1024)S(1)}, f32[4096]{0:T(1024)}, u32[]{:S(2)}) copy-start(f32[4096]{0:T(1024)} %param.21) | copy-start | bytes 49156
  183.4 162.3 %copy-start.9 = (bf16[256,4096]{1,0:T(8,128)(2,1)S(1)}, bf16[256,4096]{1,0:T(8,128)(2,1)}, u32[]{:S(2)}) copy-start(bf16[256,4096]{1,0:T(8,128)(2,1)} %param.20) | copy-start | bytes 6291460
  297.7 48.1 %collective-permute-start = (bf16[256,4096]{1,0:T(8,128)(2,1)}, bf16[256,4096]{1,0:T(8,128)(2,1)}, u32[]{:S(2)}, u32[]{:S(2)}) collective-permute-start(bf16[256,4096]{1,0:T(8,128)(2,1)} %convolution_convert_fusion), channel_id=1, source_target_pairs={{0,1},{1,0},{2,3},{3,2},{4,5},{5,4},{6,7},{7,6},{8,9},{9,8},{10,11... | collective-permute-start | bytes 6291464 | tf_op jit(solution)/shard_map/ppermute | solution.py:227
  362.7 3.5 copy-start.7
  363.5 4.9 copy-start.3
  368.4 47.0 %collective-permute-start.1 = (bf16[256,4096]{1,0:T(8,128)(2,1)S(1)}, bf16[256,4096]{1,0:T(8,128)(2,1)S(1)}, u32[]{:S(2)}, u32[]{:S(2)}) collective-permute-start(bf16[256,4096]{1,0:T(8,128)(2,1)S(1)} %get-tuple-element.7), channel_id=1, source_target_pairs={{0,1},{1,0},{2,3},{3,2},{4,5},{5,4},{6,7},{7,6},{8,9},{9,8},{10,11... | collective-permute-start | bytes 6291464 | tf_op jit(solution)/shard_map/ppermute | solution.py:227
Sparse Core Ops, SparseCore 0:
  9.5 270.0 all-gather.3
  281.8 125.7 all-gather.7
  409.8 125.0 all-gather.5

commit v2 on v1

--- a/solution.py
+++ b/solution.py
@@ -10,7 +10,7 @@
 SPAN = 256
 EXTRA = 16
 VMEM_LIMIT = 48 * 1024 * 1024
-IN_CHUNKS = 2
+IN_CHUNKS = 1
 
 
 def expand(values, width):
@@ -59,14 +59,95 @@
         sent_ref[i, state_width : state_width + EXTRA, :] = marks[:, i * lanes : (i + 1) * lanes]
 
 
+def decay_of(marks):
+    marks = marks.astype(jnp.float32)
+    return marks[0:1, :] + marks[1:2, :]
+
+
+def pair_kernel(core_ref, own_ref, other_ref, chip_ref, first_ref):
+    slices, rows, lanes = own_ref.shape
+    state_width = rows - EXTRA
+    is_first = core_ref[0] == 0
+    row = lax.broadcasted_iota(jnp.int32, (EXTRA, lanes), 0)
+    for i in range(slices):
+        own, other = own_ref[i], other_ref[i]
+        first = jnp.where(is_first, own.astype(jnp.float32), other.astype(jnp.float32))
+        second = jnp.where(is_first, other.astype(jnp.float32), own.astype(jnp.float32))
+        first_ref[i, :, :] = first.astype(jnp.bfloat16)
+        decay = decay_of(second[state_width:, :])
+        state = decay * first[:state_width, :] + second[:state_width, :]
+        chip_ref[i, 0:state_width, :] = state.astype(jnp.bfloat16)
+        whole = jnp.broadcast_to(decay * decay_of(first[state_width:, :]), (EXTRA, lanes))
+        high = whole.astype(jnp.bfloat16).astype(jnp.float32)
+        marks = jnp.where(row == 0, high, jnp.where(row == 1, whole - high, 0.0))
+        chip_ref[i, state_width:rows, :] = marks.astype(jnp.bfloat16)
+
+
 def scan_kernel(sent_ref, out_ref):
     devices, state_width, lanes = out_ref.shape
     carry = jnp.zeros((state_width, lanes), jnp.float32)
     for k in range(devices):
         out_ref[k, :, :] = carry.astype(jnp.bfloat16)
-        marks = sent_ref[k, state_width : state_width + EXTRA, :].astype(jnp.float32)
-        decay = marks[0:1, :] + marks[1:2, :]
+        decay = decay_of(sent_ref[k, state_width : state_width + EXTRA, :])
         carry = decay * carry + sent_ref[k, 0:state_width, :].astype(jnp.float32)
+
+
+def split_kernel(core_ref, start_ref, first_ref, own_ref, other_ref):
+    slices, state_width, _ = start_ref.shape
+    is_first = core_ref[0] == 0
+    for i in range(slices):
+        start = start_ref[i].astype(jnp.float32)
+        decay = decay_of(first_ref[i, state_width : state_width + EXTRA, :])
+        later = decay * start + first_ref[i, 0:state_width, :].astype(jnp.float32)
+        own_ref[i, :, :] = jnp.where(is_first, start, later).astype(jnp.bfloat16)
+        other_ref[i, :, :] = jnp.where(is_first, later, start).astype(jnp.bfloat16)
+
+
+def exchange(sent, devices):
+    chips = devices // 2
+    _, rows, lanes = sent.shape
+    state_width = rows - EXTRA
+    core = lax.rem(lax.axis_index("seq"), 2)
+    core_arg = jnp.reshape(core, (1,)).astype(jnp.int32)
+    pairs = [(i, i + 1 - 2 * (i % 2)) for i in range(devices)]
+    groups = [list(range(parity, devices, 2)) for parity in range(2)]
+    params = pltpu.CompilerParams(vmem_limit_bytes=VMEM_LIMIT)
+    vmem = pl.BlockSpec(memory_space=pltpu.VMEM)
+    smem = pl.BlockSpec(memory_space=pltpu.SMEM)
+    marked = jax.ShapeDtypeStruct((chips, rows, lanes), jnp.bfloat16)
+    plain = jax.ShapeDtypeStruct((chips, state_width, lanes), jnp.bfloat16)
+    own = lax.dynamic_slice_in_dim(sent, core * chips, chips, 0)
+    away = lax.dynamic_slice_in_dim(sent, (1 - core) * chips, chips, 0)
+    other = lax.ppermute(away, "seq", pairs)
+    chip, first = pl.pallas_call(
+        pair_kernel,
+        in_specs=[smem, vmem, vmem],
+        out_specs=[vmem, vmem],
+        out_shape=[marked, marked],
+        compiler_params=params,
+        name="chip_states",
+    )(core_arg, own, other)
+    gathered = lax.all_to_all(chip, "seq", 0, 0, axis_index_groups=groups, tiled=True)
+    starts = pl.pallas_call(
+        scan_kernel,
+        in_specs=[vmem],
+        out_specs=vmem,
+        out_shape=plain,
+        compiler_params=params,
+        name="state_scan",
+    )(gathered)
+    entering = lax.all_to_all(starts, "seq", 0, 0, axis_index_groups=groups, tiled=True)
+    mine, theirs = pl.pallas_call(
+        split_kernel,
+        in_specs=[smem, vmem, vmem],
+        out_specs=[vmem, vmem],
+        out_shape=[plain, plain],
+        compiler_params=params,
+        name="core_states",
+    )(core_arg, entering, first)
+    received = lax.ppermute(theirs, "seq", pairs)
+    both = jnp.where(core == 0, jnp.stack([mine, received]), jnp.stack([received, mine]))
+    return both.reshape(devices, state_width, lanes)
 
 
 def output_kernel(
@@ -158,16 +239,7 @@
         compiler_params=params,
         name="block_states",
     )(xin, b_flat, cum_g)
-    gathered = lax.all_to_all(sent, "seq", 0, 0, tiled=True)
-    starts = pl.pallas_call(
-        scan_kernel,
-        in_specs=[pl.BlockSpec(memory_space=pltpu.VMEM)],
-        out_specs=pl.BlockSpec(memory_space=pltpu.VMEM),
-        out_shape=jax.ShapeDtypeStruct((devices, state_width, lanes), jnp.bfloat16),
-        compiler_params=params,
-        name="state_scan",
-    )(gathered)
-    incoming = lax.all_to_all(starts, "seq", 0, 0, tiled=True)
+    incoming = exchange(sent, devices)
     row_spec = pl.BlockSpec((1, group_lanes), lambda g: (0, g))
     return pl.pallas_call(
         functools.partial(output_kernel, blocks, width),

time: 558 us -> 434 us (0.78)
  waiting for transfers between devices: 345 us -> 222 us
    all_gather x2 -> x1, waiting for transfers between devices: 104 us -> 30.7 us  [body(): lax.all_gather(w_in[:, i * in_lanes:(i + 1) * in_lanes], 'seq', axis=0, t...]
    all_to_all x1 -> x0, waiting for transfers between devices: 51.9 us -> none  [mixer(): incoming = lax.all_to_all(starts, 'seq', 0, 0, tiled=True)]
    all_to_all x1 -> x2, blocking collectives: 82.9 us -> 87.8 us  [the longest x1 46.9 us: exchange(): lax.all_to_all(chip, 'seq', 0, 0, axis_index_groups=groups, tiled=True)]
    dot_general x2 -> x1, matrix products: 27.5 us -> 23.6 us  [body(): jnp.dot(all_rows, weight, preferred_element_type=jnp.float32)]
  transfers between devices with their start and end apart: 6 -> 6, of which waited for: 5 -> 6; matrix products, arithmetic and copies ran while one was open for 11% -> 12% of each run, Pallas kernels for 5% -> 6%
where the time goes in v2:
time: 434 us; the launch traced here: 433 us
  waiting for transfers between devices  222 us (51%)
  blocking collectives  87.8 us (20%)
  matrix products  59.6 us (14%)
  Pallas kernels  28 us (6%)
  between operations  15 us (3%)
  local copies, waits for them, and re-layouts  11 us (3%)
  other arithmetic  6.17 us (1%)
    all_gather x1, waiting for transfers between devices, body(): w_out_all = lax.all_gather(w_out, 'seq', axis=1, tiled=True)  95.7 us
    ppermute x2, waiting for transfers between devices, shift(): return lax.ppermute(array, 'head', pairs)  90.7 us
    all_to_all x1, blocking collectives, exchange(): lax.all_to_all(chip, 'seq', 0, 0, axis_index_groups=groups, tiled=True)  46.9 us
    all_to_all x1, blocking collectives, exchange(): lax.all_to_all(starts, 'seq', 0, 0, axis_index_groups=groups, tiled=True)  40.9 us
    dot_general x2, matrix products, partial_of(): jnp.dot(rows, w_out_all, preferred_element_type=jnp.float32)  35.6 us
    all_gather x1, waiting for transfers between devices, body(): lax.all_gather(w_in[:, i * in_lanes:(i + 1) * in_lanes], 'seq', axis=0, t...  30.7 us
    dot_general x1, matrix products, body(): jnp.dot(all_rows, weight, preferred_element_type=jnp.float32)  23.6 us
    pallas_call x1, Pallas kernels, mixer(): pl.pallas_call(functools.partial(output_kernel, blocks, width), grid=(gro...  17.9 us
  transfers between devices with their start and end apart: 6, of which 6 were waited for; matrix products, arithmetic and copies ran while one was open for 12% of the time, Pallas kernels for 6%

profile of v2, /device:TPU:0, one launch (start us, length us, event | category | flops | bytes accessed | tf_op | source)
XLA Modules:
  0.0 433.3 jit_solution(471681869092926041)
XLA Ops:
  7.2 0.0 copy-start.5
  7.2 0.0 copy-start.4
  7.2 0.0 all-gather.3.cloned.1.call-start
  7.2 0.7 all-gather.3.cloned.1.call-update
  7.9 0.0 all-gather.5.cloned.1.call-start
  8.0 0.7 all-gather.5.cloned.1.call-update
  8.7 0.0 copy-done.5
  8.7 0.4 fusion.8
  9.1 0.1 copy.15
  9.2 0.1 reshape.38
  9.3 0.3 copy.17.cum_ref
  9.7 0.0 copy-done.4
  9.7 0.2 copy.19
  9.9 7.7 %block_states.1 = (bf16[16,272,256]{2,1,0:T(8,128)(2,1)}, bf16[1,256,4096]{2,1,0:T(8,128)(2,1)S(1)}) custom-call(bf16[512,4096]{1,0:T(8,128)(2,1)} %x_ref.3, bf16[512,1024]{1,0:T(8,128)(2,1)S(1)} %bitcast.28, f32[4,512,16]{2,1,0:T(8,128)S(1)} %copy.17.cum_ref), custom_call_target="tpu_custom_call" | custom-call | tf_op jit(solution)/shard_map/block_states/pallas_call | solution.py:227
  17.7 0.0 copy-start
  17.7 1.3 copy-done
  19.0 2.0 constant_dynamic-slice_fusion
  21.0 0.5 collective-permute-start
  21.5 2.4 collective-permute-done.other_ref
  23.8 0.8 chip_states.1
  24.6 46.9 %all_to_all.10.sent_ref = bf16[8,272,256]{2,1,0:T(8,128)(2,1)S(1)} all-to-all(bf16[8,272,256]{2,1,0:T(8,128)(2,1)S(1)} %get-tuple-element.9), channel_id=1, replica_groups={{0,4,8,12,16,20,24,28},{2,6,10,14,18,22,26,30},{1,5,9,13,17,21,25,29},{..., dimensions={0} | all-to-all | bytes 2228224 | tf_op jit(solution)/shard_map/all_to_all | solution.py:130
  71.5 0.0 copy-start.8
  71.5 0.2 state_scan.1
  71.7 40.9 %all_to_all.11.start_ref = bf16[8,256,256]{2,1,0:T(8,128)(2,1)S(1)} all-to-all(bf16[8,256,256]{2,1,0:T(8,128)(2,1)S(1)} %state_scan.1), channel_id=1, replica_groups={{0,4,8,12,16,20,24,28},{2,6,10,14,18,22,26,30},{1,5,9,13,17,21,25,29},{..., dimensions={0} | all-to-all | bytes 2097152 | tf_op jit(solution)/shard_map/all_to_all | solution.py:139
  112.6 0.0 copy-start.2
  112.6 1.4 core_states.1
  114.0 0.0 copy-start.1
  114.0 1.0 copy-done.1
  115.0 0.0 collective-permute-start.1
  115.0 1.4 copy.20
  116.4 0.0 copy-done.8
  116.5 0.1 broadcast_in_dim.23
  116.5 0.1 broadcast_in_dim_reshape.3.skip_ref
  116.6 1.4 collective-permute-done.1
  118.0 2.6 maximum_select_fusion
  120.6 0.0 copy-done.2
  120.6 17.9 %mixer_out.1 = bf16[512,4096]{1,0:T(8,128)(2,1)} custom-call(bf16[512,4096]{1,0:T(8,128)(2,1)} %x_ref.3, bf16[512,4096]{1,0:T(8,128)(2,1)} %z_ref.1, bf16[512,1024]{1,0:T(8,128)(2,1)S(1)} %bitcast.29, bf16[512,1024]{1,0:T(8,128)(2,1)S(1)} %bitcast.31, f32[4,512,16]{2,1,0:T(8,128)S(1)} %copy.17.cum_ref, f32[4,16,512]{2,1,0:T(8,128)S(1)} %bitcast.33, ...), custom_call_target="tpu_custom_call" | custom-call | tf_op jit(solution)/shard_map/mixer_out/pallas_call | solution.py:244
  138.5 0.0 copy-start.6
  138.5 0.0 copy-start.9
  138.5 95.7 %all-gather.3.cloned.1.call-done = bf16[4096,4096]{1,0:T(8,128)(2,1)} async-done(((bf16[4096,256]{1,0:T(8,128)(2,1)}), bf16[4096,4096]{1,0:T(8,128)(2,1)}) %all-gather.3.cloned.1.call-update) | async-done | bytes 33554448 | tf_op jit(solution)/shard_map/all_gather | solution.py:301
  234.2 18.4 %convolution_convert_fusion.1 = bf16[256,4096]{1,0:T(8,128)(2,1)} fusion(bf16[4096,4096]{1,0:T(8,128)(2,1)} %all-gather.3.cloned.1.call-done, bf16[512,4096]{1,0:T(8,128)(2,1)} %mixer_out.1, s32[]{:T(128)S(6)} %select_n.39), kind=kOutput, calls=%fused_computation.3 | convolution fusion | flops 8590983168 | bytes 37748740 | tf_op jit(solution)/shard_map/dot_general | solution.py:311
  252.5 1.5 collective-permute-start.2
  254.0 0.0 copy-done.6
  254.0 0.7 multiply_reduce_fusion.1
  255.4 45.2 %collective-permute-done.2 = bf16[256,4096]{1,0:T(8,128)(2,1)} collective-permute-done((bf16[256,4096]{1,0:T(8,128)(2,1)}, bf16[256,4096]{1,0:T(8,128)(2,1)}, u32[]{:S(2)}, u32[]{:S(2)}) %collective-permute-start.2) | collective-permute-done | bytes 2097184 | tf_op jit(solution)/shard_map/ppermute | solution.py:299
  300.6 0.0 copy-done.9
  300.6 17.2 %multiply_reduce_fusion = (f32[256]{0:T(256)S(1)}, f32[256,4096]{1,0:T(8,128)S(1)}) fusion(f32[4096]{0:T(1024)S(1)} %broadcast_divide_fusion, bf16[256,4096]{1,0:T(8,128)(2,1)} %collective-permute-done.2, bf16[4096,4096]{1,0:T(8,128)(2,1)} %all-gather.3.cloned.1.call-done, bf16[512,4096]{1,0:T(8,128)(2,1)} %mixer_out.1, s32[]{:T(128)S(6)} %select_n.38, ...), kind=kOutput, calls=%fused_computation.10 | convolution fusion | flops 8598323200 | bytes 44057604 | tf_op jit(solution)/shard_map/dot_general | solution.py:311
  317.9 0.0 copy-start.7
  317.9 0.8 fusion.1
  318.7 0.0 copy-start.3
  318.7 2.8 broadcast_in_dim.25
  321.4 0.0 copy-done.7
  321.4 2.1 constant_dynamic-update-slice_fusion.1
  323.6 0.0 copy-done.3
  323.6 1.6 collective-permute-start.3
  325.2 45.5 %collective-permute-done.3 = bf16[256,4096]{1,0:T(8,128)(2,1)S(1)} collective-permute-done((bf16[256,4096]{1,0:T(8,128)(2,1)S(1)}, bf16[256,4096]{1,0:T(8,128)(2,1)S(1)}, u32[]{:S(2)}, u32[]{:S(2)}) %collective-permute-start.3) | collective-permute-done | bytes 2097184 | tf_op jit(solution)/shard_map/ppermute | solution.py:299
  370.6 1.5 constant_dynamic-update-slice_fusion
  372.2 30.7 %all-gather.5.cloned.1.call-done = bf16[4096,4096]{1,0:T(8,128)(2,1)} async-done(((bf16[256,4096]{1,0:T(8,128)(2,1)}), bf16[4096,4096]{1,0:T(8,128)(2,1)}) %all-gather.5.cloned.1.call-update) | async-done | bytes 33554448 | tf_op jit(solution)/shard_map/all_gather | solution.py:304
  402.9 23.6 %convolution_convert_fusion = bf16[512,4096]{1,0:T(8,128)(2,1)} fusion(bf16[512,4096]{1,0:T(8,128)(2,1)} %constant_dynamic-update-slice_fusion, bf16[4096,4096]{1,0:T(8,128)(2,1)} %all-gather.5.cloned.1.call-done), kind=kOutput, calls=%fused_computation | convolution fusion | flops 17181966336 | bytes 41943040 | tf_op jit(solution)/shard_map/dot_general | solution.py:336
  (3 shorter events, 0.0 us)
Async XLA Ops:
  7.2 1.5 copy-start.5
  7.2 2.5 copy-start.4
  7.2 227.0 %all-gather.3.cloned.1.call-start = ((), (), s32[]{:S(2)}) async-start(), calls=%async_computation.2 | async-start | bytes 35651584 | tf_op jit(solution)/shard_map/all_gather | solution.py:301
  7.9 395.0 %all-gather.5.cloned.1.call-start = ((), (), s32[]{:S(2)}) async-start(), calls=%async_computation.3 | async-start | bytes 35651584 | tf_op jit(solution)/shard_map/all_gather | solution.py:304
  17.7 1.3 copy-start
  21.0 2.9 collective-permute-start
  71.5 44.9 %copy-start.8 = (f32[64]{0:T(128)S(1)}, f32[64]{0:T(128)}, u32[]{:S(2)}) copy-start(f32[64]{0:T(128)} %param.17) | copy-start | bytes 772
  112.6 8.0 %copy-start.2 = (f32[4096]{0:T(1024)S(1)}, f32[4096]{0:T(1024)}, u32[]{:S(2)}) copy-start(f32[4096]{0:T(1024)} %param.18) | copy-start | bytes 49156
  114.0 1.0 copy-start.1
  115.0 3.0 collective-permute-start.1
  138.5 115.5 %copy-start.6 = (f32[4096]{0:T(1024)S(1)}, f32[4096]{0:T(1024)}, u32[]{:S(2)}) copy-start(f32[4096]{0:T(1024)} %param.21) | copy-start | bytes 49156
  138.5 162.2 %copy-start.9 = (bf16[256,4096]{1,0:T(8,128)(2,1)S(1)}, bf16[256,4096]{1,0:T(8,128)(2,1)}, u32[]{:S(2)}) copy-start(bf16[256,4096]{1,0:T(8,128)(2,1)} %param.20) | copy-start | bytes 6291460
  252.5 48.1 %collective-permute-start.2 = (bf16[256,4096]{1,0:T(8,128)(2,1)}, bf16[256,4096]{1,0:T(8,128)(2,1)}, u32[]{:S(2)}, u32[]{:S(2)}) collective-permute-start(bf16[256,4096]{1,0:T(8,128)(2,1)} %convolution_convert_fusion.1), channel_id=1, source_target_pairs={{0,1},{1,0},{2,3},{3,2},{4,5},{5,4},{6,7},{7,6},{8,9},{9,8},{10,11... | collective-permute-start | bytes 6291464 | tf_op jit(solution)/shard_map/ppermute | solution.py:299
  317.9 3.6 copy-start.7
  318.7 4.9 %copy-start.3 = (bf16[256,4096]{1,0:T(8,128)(2,1)}, bf16[256,4096]{1,0:T(8,128)(2,1)S(1)}, u32[]{:S(2)}) copy-start(bf16[256,4096]{1,0:T(8,128)(2,1)S(1)} %get-tuple-element.17) | copy-start | bytes 6291460
  323.6 47.0 %collective-permute-start.3 = (bf16[256,4096]{1,0:T(8,128)(2,1)S(1)}, bf16[256,4096]{1,0:T(8,128)(2,1)S(1)}, u32[]{:S(2)}, u32[]{:S(2)}) collective-permute-start(bf16[256,4096]{1,0:T(8,128)(2,1)S(1)} %get-tuple-element.15), channel_id=1, source_target_pairs={{0,1},{1,0},{2,3},{3,2},{4,5},{5,4},{6,7},{7,6},{8,9},{9,8},{10,11... | collective-permute-start | bytes 6291464 | tf_op jit(solution)/shard_map/ppermute | solution.py:299
Sparse Core Ops, SparseCore 0:
  9.5 224.5 all-gather.2
  235.8 167.0 all-gather.4

commit v3 on v2

--- a/solution.py
+++ b/solution.py
@@ -10,7 +10,7 @@
 SPAN = 256
 EXTRA = 16
 VMEM_LIMIT = 48 * 1024 * 1024
-IN_CHUNKS = 1
+TILE = 512
 
 
 def expand(values, width):
@@ -64,10 +64,10 @@
     return marks[0:1, :] + marks[1:2, :]
 
 
-def pair_kernel(core_ref, own_ref, other_ref, chip_ref, first_ref):
+def pair_kernel(side_ref, own_ref, other_ref, pair_ref, first_ref):
     slices, rows, lanes = own_ref.shape
     state_width = rows - EXTRA
-    is_first = core_ref[0] == 0
+    is_first = side_ref[0] == 0
     row = lax.broadcasted_iota(jnp.int32, (EXTRA, lanes), 0)
     for i in range(slices):
         own, other = own_ref[i], other_ref[i]
@@ -76,25 +76,16 @@
         first_ref[i, :, :] = first.astype(jnp.bfloat16)
         decay = decay_of(second[state_width:, :])
         state = decay * first[:state_width, :] + second[:state_width, :]
-        chip_ref[i, 0:state_width, :] = state.astype(jnp.bfloat16)
+        pair_ref[i, 0:state_width, :] = state.astype(jnp.bfloat16)
         whole = jnp.broadcast_to(decay * decay_of(first[state_width:, :]), (EXTRA, lanes))
         high = whole.astype(jnp.bfloat16).astype(jnp.float32)
         marks = jnp.where(row == 0, high, jnp.where(row == 1, whole - high, 0.0))
-        chip_ref[i, state_width:rows, :] = marks.astype(jnp.bfloat16)
-
-
-def scan_kernel(sent_ref, out_ref):
-    devices, state_width, lanes = out_ref.shape
-    carry = jnp.zeros((state_width, lanes), jnp.float32)
-    for k in range(devices):
-        out_ref[k, :, :] = carry.astype(jnp.bfloat16)
-        decay = decay_of(sent_ref[k, state_width : state_width + EXTRA, :])
-        carry = decay * carry + sent_ref[k, 0:state_width, :].astype(jnp.float32)
-
-
-def split_kernel(core_ref, start_ref, first_ref, own_ref, other_ref):
+        pair_ref[i, state_width:rows, :] = marks.astype(jnp.bfloat16)
+
+
+def split_kernel(side_ref, start_ref, first_ref, own_ref, other_ref):
     slices, state_width, _ = start_ref.shape
-    is_first = core_ref[0] == 0
+    is_first = side_ref[0] == 0
     for i in range(slices):
         start = start_ref[i].astype(jnp.float32)
         decay = decay_of(first_ref[i, state_width : state_width + EXTRA, :])
@@ -103,51 +94,44 @@
         other_ref[i, :, :] = jnp.where(is_first, later, start).astype(jnp.bfloat16)
 
 
-def exchange(sent, devices):
-    chips = devices // 2
-    _, rows, lanes = sent.shape
+def exchange(sent, devices, reach=1):
+    slices, rows, lanes = sent.shape
+    half = slices // 2
     state_width = rows - EXTRA
-    core = lax.rem(lax.axis_index("seq"), 2)
-    core_arg = jnp.reshape(core, (1,)).astype(jnp.int32)
-    pairs = [(i, i + 1 - 2 * (i % 2)) for i in range(devices)]
-    groups = [list(range(parity, devices, 2)) for parity in range(2)]
+    side = lax.rem(lax.axis_index("seq") // reach, 2)
+    side_arg = jnp.reshape(side, (1,)).astype(jnp.int32)
+    pairs = [(i, i ^ reach) for i in range(devices)]
     params = pltpu.CompilerParams(vmem_limit_bytes=VMEM_LIMIT)
     vmem = pl.BlockSpec(memory_space=pltpu.VMEM)
     smem = pl.BlockSpec(memory_space=pltpu.SMEM)
-    marked = jax.ShapeDtypeStruct((chips, rows, lanes), jnp.bfloat16)
-    plain = jax.ShapeDtypeStruct((chips, state_width, lanes), jnp.bfloat16)
-    own = lax.dynamic_slice_in_dim(sent, core * chips, chips, 0)
-    away = lax.dynamic_slice_in_dim(sent, (1 - core) * chips, chips, 0)
+    marked = jax.ShapeDtypeStruct((half, rows, lanes), jnp.bfloat16)
+    plain = jax.ShapeDtypeStruct((half, state_width, lanes), jnp.bfloat16)
+    own = lax.dynamic_slice_in_dim(sent, side * half, half, 0)
+    away = lax.dynamic_slice_in_dim(sent, (1 - side) * half, half, 0)
     other = lax.ppermute(away, "seq", pairs)
-    chip, first = pl.pallas_call(
+    pair, first = pl.pallas_call(
         pair_kernel,
         in_specs=[smem, vmem, vmem],
         out_specs=[vmem, vmem],
         out_shape=[marked, marked],
         compiler_params=params,
-        name="chip_states",
-    )(core_arg, own, other)
-    gathered = lax.all_to_all(chip, "seq", 0, 0, axis_index_groups=groups, tiled=True)
-    starts = pl.pallas_call(
-        scan_kernel,
-        in_specs=[vmem],
-        out_specs=vmem,
-        out_shape=plain,
-        compiler_params=params,
-        name="state_scan",
-    )(gathered)
-    entering = lax.all_to_all(starts, "seq", 0, 0, axis_index_groups=groups, tiled=True)
+        name=f"pair_{reach}",
+    )(side_arg, own, other)
+    if 2 * reach < devices:
+        entering = exchange(pair, devices, 2 * reach)
+    else:
+        entering = jnp.zeros(plain.shape, plain.dtype)
     mine, theirs = pl.pallas_call(
         split_kernel,
         in_specs=[smem, vmem, vmem],
         out_specs=[vmem, vmem],
         out_shape=[plain, plain],
         compiler_params=params,
-        name="core_states",
-    )(core_arg, entering, first)
+        name=f"split_{reach}",
+    )(side_arg, entering, first)
     received = lax.ppermute(theirs, "seq", pairs)
-    both = jnp.where(core == 0, jnp.stack([mine, received]), jnp.stack([received, mine]))
-    return both.reshape(devices, state_width, lanes)
+    both = jnp.where(side == 0, jnp.stack([mine, received]), jnp.stack([received, mine]))
+    return both.reshape(slices, state_width, lanes)
 
 
 def output_kernel(
@@ -274,6 +258,35 @@
     )
 
 
+def product_kernel(rows_ref, weight_ref, out_ref):
+    out_ref[...] = jnp.dot(
+        rows_ref[...], weight_ref[...], preferred_element_type=jnp.float32
+    ).astype(jnp.bfloat16)
+
+
+def product(rows, weight):
+    count, depth = rows.shape
+    columns = weight.shape[1]
+    tile = min(TILE, columns)
+    return pl.pallas_call(
+        product_kernel,
+        grid=(columns // tile,),
+        in_specs=[
+            pl.BlockSpec((count, depth), lambda j: (0, 0)),
+            pl.BlockSpec((depth, tile), lambda j: (0, j)),
+        ],
+        out_specs=pl.BlockSpec((count, tile), lambda j: (0, j)),
+        out_shape=jax.ShapeDtypeStruct((count, columns), jnp.bfloat16),
+        compiler_params=pltpu.CompilerParams(vmem_limit_bytes=VMEM_LIMIT),
+        cost_estimate=pl.CostEstimate(
+            flops=2 * count * depth * columns,
+            bytes_accessed=2 * (count * depth + depth * columns + count * columns),
+            transcendentals=0,
+        ),
+        name="next_x",
+    )(rows, weight)
+
+
 def body(
     xin,
     gate_z,
@@ -299,11 +312,7 @@
         return lax.ppermute(array, "head", pairs)
 
     w_out_all = lax.all_gather(w_out, "seq", axis=1, tiled=True)
-    in_lanes = w_in.shape[1] // IN_CHUNKS
-    w_in_all = [
-        lax.all_gather(w_in[:, i * in_lanes : (i + 1) * in_lanes], "seq", axis=0, tiled=True)
-        for i in range(IN_CHUNKS)
-    ]
+    w_in_all = lax.all_gather(w_in, "seq", axis=0, tiled=True)
     ssd_out = mixer(xin, gate_z, b_proj, c_proj, log_retain, skip_d, norm_gain, devices)
 
     def partial_of(index):
@@ -331,13 +340,7 @@
         rows = normed if by == 0 else shift(normed, by)
         source = lax.rem(place - by + head_devices, head_devices)
         all_rows = lax.dynamic_update_slice_in_dim(all_rows, rows, source * own_rows, 0)
-    next_x = jnp.concatenate(
-        [
-            jnp.dot(all_rows, weight, preferred_element_type=jnp.float32).astype(jnp.bfloat16)
-            for weight in w_in_all
-        ],
-        axis=1,
-    )
+    next_x = product(all_rows, w_in_all)
     return (stream, next_x)
 
 

time: 434 us -> 422 us (0.972)
  blocking collectives: 87.8 us -> 0 us
  waiting for transfers between devices: 222 us -> 273 us
  Pallas kernels: 28 us -> 55.9 us
  matrix products: 59.6 us -> 35.9 us
  local copies, waits for them, and re-layouts: 11 us -> 20.8 us
  starting transfers between devices: 3.6 us -> 11.2 us
    all_to_all x2 -> x0, blocking collectives: 87.8 us -> none  [the longest x1 46.9 us: exchange(): lax.all_to_all(chip, 'seq', 0, 0, axis_index_groups=groups, tiled=True)]
    ppermute x1 -> x4, waiting for transfers between devices: 2.38 us -> 49.6 us  [exchange(): other = lax.ppermute(away, 'seq', pairs)]
    all_gather x1, waiting for transfers between devices: 95.7 us -> 50.1 us  [body(): w_out_all = lax.all_gather(w_out, 'seq', axis=1, tiled=True)]
    ppermute x1 -> x4, waiting for transfers between devices: 1.36 us -> 44 us  [exchange(): received = lax.ppermute(theirs, 'seq', pairs)]
    dot_general x1 -> x0, matrix products: 23.6 us -> none  [body(): jnp.dot(all_rows, weight, preferred_element_type=jnp.float32)]
    pallas_call x1, Pallas kernels: 0.21 us -> 21.8 us  [product(): pl.pallas_call(product_kernel, grid=(columns // tile,), in_specs=[pl.Bloc...]
    unnamed x22 -> x44, local copies, waits for them, and re-layouts: 4.03 us -> 14.5 us
    ppermute x1 -> x4, starting transfers between devices: 0.48 us -> 5.92 us  [exchange(): other = lax.ppermute(away, 'seq', pairs)]
  transfers between devices with their start and end apart: 6 -> 12, of which waited for: 6 -> 12; matrix products, arithmetic and copies ran while one was open for 12% -> 13% of each run, Pallas kernels for 6% -> 8%
where the time goes in v3:
time: 422 us; the launch traced here: 421 us
  waiting for transfers between devices  273 us (65%)
  Pallas kernels  55.9 us (13%)
  matrix products  35.9 us (9%)
  local copies, waits for them, and re-layouts  20.8 us (5%)
  between operations  15.1 us (4%)
  starting transfers between devices  11.2 us (3%)
  other arithmetic  9.11 us (2%)
    ppermute x2, waiting for transfers between devices, shift(): return lax.ppermute(array, 'head', pairs)  93.4 us
    all_gather x1, waiting for transfers between devices, body(): w_out_all = lax.all_gather(w_out, 'seq', axis=1, tiled=True)  50.1 us
    ppermute x4, waiting for transfers between devices, exchange(): other = lax.ppermute(away, 'seq', pairs)  49.6 us
    ppermute x4, waiting for transfers between devices, exchange(): received = lax.ppermute(theirs, 'seq', pairs)  44 us
    dot_general x2, matrix products, partial_of(): jnp.dot(rows, w_out_all, preferred_element_type=jnp.float32)  35.5 us
    all_gather x1, waiting for transfers between devices, body(): w_in_all = lax.all_gather(w_in, 'seq', axis=0, tiled=True)  35 us
    pallas_call x1, Pallas kernels, product(): pl.pallas_call(product_kernel, grid=(columns // tile,), in_specs=[pl.Bloc...  21.8 us
    pallas_call x1, Pallas kernels, mixer(): pl.pallas_call(functools.partial(output_kernel, blocks, width), grid=(gro...  18.2 us
  transfers between devices with their start and end apart: 12, of which 12 were waited for; matrix products, arithmetic and copies ran while one was open for 13% of the time, Pallas kernels for 8%

profile of v3, /device:TPU:0, one launch (start us, length us, event | category | flops | bytes accessed | tf_op | source)
XLA Modules:
  0.0 421.5 jit_solution(6700048126888516109)
XLA Ops:
  7.2 0.7 all-gather.3.cloned.1.call-update
  8.0 0.7 all-gather.5.cloned.1.call-update
  8.7 0.4 fusion.8
  9.1 0.1 copy.15
  9.2 0.1 reshape.83
  9.3 0.3 copy.17.cum_ref
  9.7 0.2 copy.19
  9.9 7.7 %block_states.1 = (bf16[16,272,256]{2,1,0:T(8,128)(2,1)}, bf16[1,256,4096]{2,1,0:T(8,128)(2,1)S(1)}) custom-call(bf16[512,4096]{1,0:T(8,128)(2,1)} %x_ref.3, bf16[512,1024]{1,0:T(8,128)(2,1)S(1)} %bitcast.35, f32[4,512,16]{2,1,0:T(8,128)S(1)} %copy.17.cum_ref), custom_call_target="tpu_custom_call" | custom-call | tf_op jit(solution)/shard_map/block_states/pallas_call | solution.py:211
  17.7 1.3 copy-done.2
  19.0 3.0 constant_dynamic-slice_fusion.6
  22.0 0.4 collective-permute-start
  22.4 2.7 collective-permute-done.other_ref
  25.1 2.0 pair_1.1
  27.2 1.0 copy-done.3
  28.1 0.9 constant_dynamic-slice_fusion.4
  29.0 2.7 collective-permute-start.1
  31.7 25.2 %collective-permute-done.1.other_ref = bf16[4,272,256]{2,1,0:T(8,128)(2,1)S(1)} collective-permute-done((bf16[4,272,256]{2,1,0:T(8,128)(2,1)}, bf16[4,272,256]{2,1,0:T(8,128)(2,1)S(1)}, u32[]{:S(2)}, u32[]{:S(2)}) %collective-permute-start.1) | collective-permute-done | bytes 557088 | tf_op jit(solution)/shard_map/ppermute | solution.py:111
  57.0 0.4 pair_2.1
  57.4 0.9 constant_dynamic-slice_fusion.2
  58.3 0.1 copy-done.7
  58.4 15.3 %collective-permute-done.2.other_ref = bf16[2,272,256]{2,1,0:T(8,128)(2,1)} collective-permute-done((bf16[2,272,256]{2,1,0:T(8,128)(2,1)}, bf16[2,272,256]{2,1,0:T(8,128)(2,1)}, u32[]{:S(2)}, u32[]{:S(2)}) %collective-permute-start.2) | collective-permute-done | bytes 278560 | tf_op jit(solution)/shard_map/ppermute | solution.py:111
  73.7 1.0 copy-done.5
  74.7 1.1 pair_4.1
  75.8 0.7 copy-done.10
  76.6 2.8 collective-permute-start.3
  79.4 6.3 %collective-permute-done.3.other_ref = bf16[1,272,256]{2,1,0:T(8,128)(2,1)S(1)} collective-permute-done((bf16[1,272,256]{2,1,0:T(8,128)(2,1)S(1)}, bf16[1,272,256]{2,1,0:T(8,128)(2,1)S(1)}, u32[]{:S(2)}, u32[]{:S(2)}) %collective-permute-start.3) | collective-permute-done | bytes 139296 | tf_op jit(solution)/shard_map/ppermute | solution.py:111
  85.7 0.7 pair_8.1
  86.4 0.7 split_8.1
  87.1 3.4 collective-permute-start.4
  90.5 8.5 %collective-permute-done.4 = bf16[1,256,256]{2,1,0:T(8,128)(2,1)} collective-permute-done((bf16[1,256,256]{2,1,0:T(8,128)(2,1)}, bf16[1,256,256]{2,1,0:T(8,128)(2,1)}, u32[]{:S(2)}, u32[]{:S(2)}) %collective-permute-start.4) | collective-permute-done | bytes 131104 | tf_op jit(solution)/shard_map/ppermute | solution.py:132
  99.0 1.0 maximum_select_fusion.3.start_ref
  100.1 0.9 copy-done.11
  101.0 0.8 split_4.1
  101.8 0.7 copy-done.12
  102.6 11.3 %collective-permute-done.5 = bf16[2,256,256]{2,1,0:T(8,128)(2,1)} collective-permute-done((bf16[2,256,256]{2,1,0:T(8,128)(2,1)}, bf16[2,256,256]{2,1,0:T(8,128)(2,1)}, u32[]{:S(2)}, u32[]{:S(2)}) %collective-permute-start.5) | collective-permute-done | bytes 262176 | tf_op jit(solution)/shard_map/ppermute | solution.py:132
  113.9 1.3 maximum_select_fusion.2
  115.2 1.1 copy-done.8
  116.3 1.0 split_2.1
  117.3 0.8 copy-done.9
  118.0 1.5 collective-permute-start.6
  119.6 22.8 %collective-permute-done.6 = bf16[4,256,256]{2,1,0:T(8,128)(2,1)} collective-permute-done((bf16[4,256,256]{2,1,0:T(8,128)(2,1)}, bf16[4,256,256]{2,1,0:T(8,128)(2,1)}, u32[]{:S(2)}, u32[]{:S(2)}) %collective-permute-start.6) | collective-permute-done | bytes 524320 | tf_op jit(solution)/shard_map/ppermute | solution.py:132
  142.4 1.8 maximum_select_fusion.1
  144.2 1.4 split_1.1
  145.5 1.0 copy-done.6
  146.5 1.5 copy.20
  148.1 0.1 broadcast_in_dim_reshape.3.skip_ref
  148.2 1.4 collective-permute-done.7
  149.5 2.8 maximum_select_fusion
  152.3 18.2 %mixer_out.1 = bf16[512,4096]{1,0:T(8,128)(2,1)} custom-call(bf16[512,4096]{1,0:T(8,128)(2,1)} %x_ref.3, bf16[512,4096]{1,0:T(8,128)(2,1)} %z_ref.1, bf16[512,1024]{1,0:T(8,128)(2,1)S(1)} %bitcast.36, bf16[512,1024]{1,0:T(8,128)(2,1)S(1)} %bitcast.38, f32[4,512,16]{2,1,0:T(8,128)S(1)} %copy.17.cum_ref, f32[4,16,512]{2,1,0:T(8,128)S(1)} %bitcast.42, ...), custom_call_target="tpu_custom_call" | custom-call | tf_op jit(solution)/shard_map/mixer_out/pallas_call | solution.py:228
  170.4 50.1 %all-gather.3.cloned.1.call-done = bf16[4096,4096]{1,0:T(8,128)(2,1)} async-done(((bf16[4096,256]{1,0:T(8,128)(2,1)}), bf16[4096,4096]{1,0:T(8,128)(2,1)}) %all-gather.3.cloned.1.call-update) | async-done | bytes 33554448 | tf_op jit(solution)/shard_map/all_gather | solution.py:314
  220.5 18.4 %convolution_convert_fusion = bf16[256,4096]{1,0:T(8,128)(2,1)} fusion(bf16[4096,4096]{1,0:T(8,128)(2,1)} %all-gather.3.cloned.1.call-done, bf16[512,4096]{1,0:T(8,128)(2,1)} %mixer_out.1, s32[]{:T(128)S(6)} %select_n.121), kind=kOutput, calls=%fused_computation.2 | convolution fusion | flops 8590983168 | bytes 37748740 | tf_op jit(solution)/shard_map/dot_general | solution.py:320
  238.9 0.7 multiply_reduce_fusion.1
  240.3 46.7 %collective-permute-done.8 = bf16[256,4096]{1,0:T(8,128)(2,1)} collective-permute-done((bf16[256,4096]{1,0:T(8,128)(2,1)}, bf16[256,4096]{1,0:T(8,128)(2,1)}, u32[]{:S(2)}, u32[]{:S(2)}) %collective-permute-start.8) | collective-permute-done | bytes 2097184 | tf_op jit(solution)/shard_map/ppermute | solution.py:312
  287.0 17.2 %multiply_reduce_fusion = (f32[256]{0:T(256)S(1)}, f32[256,4096]{1,0:T(8,128)S(1)}) fusion(f32[4096]{0:T(1024)S(1)} %broadcast_divide_fusion, bf16[256,4096]{1,0:T(8,128)(2,1)} %collective-permute-done.8, bf16[4096,4096]{1,0:T(8,128)(2,1)} %all-gather.3.cloned.1.call-done, bf16[512,4096]{1,0:T(8,128)(2,1)} %mixer_out.1, s32[]{:T(128)S(6)} %select_n.120, ...), kind=kOutput, calls=%fused_computation.9 | convolution fusion | flops 8598323200 | bytes 44057604 | tf_op jit(solution)/shard_map/dot_general | solution.py:320
  304.2 0.8 fusion.1
  305.0 0.5 broadcast_in_dim.29
  305.5 0.8 constant_dynamic-update-slice_fusion.1
  306.3 0.3 collective-permute-start.9
  306.6 46.7 %collective-permute-done.9 = bf16[256,4096]{1,0:T(8,128)(2,1)S(1)} collective-permute-done((bf16[256,4096]{1,0:T(8,128)(2,1)S(1)}, bf16[256,4096]{1,0:T(8,128)(2,1)S(1)}, u32[]{:S(2)}, u32[]{:S(2)}) %collective-permute-start.9) | collective-permute-done | bytes 2097184 | tf_op jit(solution)/shard_map/ppermute | solution.py:312
  353.3 0.3 constant_dynamic-update-slice_fusion.rows_ref
  353.6 2.0 copy-done
  355.6 35.0 %all-gather.5.cloned.1.call-done.weight_ref = bf16[4096,4096]{1,0:T(8,128)(2,1)} async-done(((bf16[256,4096]{1,0:T(8,128)(2,1)}), bf16[4096,4096]{1,0:T(8,128)(2,1)}) %all-gather.5.cloned.1.call-update) | async-done | bytes 33554448 | tf_op jit(solution)/shard_map/all_gather | solution.py:315
  390.7 2.2 copy-done.1
  392.9 21.8 %next_x.1 = bf16[512,4096]{1,0:T(8,128)(2,1)} custom-call(bf16[512,4096]{1,0:T(8,128)(2,1)S(1)} %copy-done.1, bf16[4096,4096]{1,0:T(8,128)(2,1)} %all-gather.5.cloned.1.call-done.weight_ref), custom_call_target="tpu_custom_call" | custom-call | flops 17179869184 | bytes 41943040 | tf_op jit(solution)/shard_map/next_x/pallas_call | solution.py:271
  (42 shorter events, 0.3 us)
Async XLA Ops:
  7.2 1.5 copy-start.16
  7.2 2.5 copy-start.15
  7.2 213.3 %all-gather.3.cloned.1.call-start = ((), (), s32[]{:S(2)}) async-start(), calls=%async_computation | async-start | bytes 35651584 | tf_op jit(solution)/shard_map/all_gather | solution.py:314
  7.9 382.7 %all-gather.5.cloned.1.call-start = ((), (), s32[]{:S(2)}) async-start(), calls=%async_computation.1 | async-start | bytes 35651584 | tf_op jit(solution)/shard_map/all_gather | solution.py:315
  17.7 1.3 copy-start.2
  22.0 3.1 collective-permute-start
  27.1 1.0 copy-start.3
  29.0 28.0 %collective-permute-start.1 = (bf16[4,272,256]{2,1,0:T(8,128)(2,1)}, bf16[4,272,256]{2,1,0:T(8,128)(2,1)S(1)}, u32[]{:S(2)}, u32[]{:S(2)}) collective-permute-start(bf16[4,272,256]{2,1,0:T(8,128)(2,1)} %get-tuple-element.42), channel_id=1, source_target_pairs={{0,4},{2,6},{4,0},{6,2},{8,12},{10,14},{12,8},{14,10},{16,20},{18,... | collective-permute-start | bytes 1671176 | tf_op jit(solution)/shard_map/ppermute | solution.py:111
  57.4 1.0 copy-start.7
  57.4 86.7 %copy-start.4 = (bf16[8,272,256]{2,1,0:T(8,128)(2,1)S(1)}, bf16[8,272,256]{2,1,0:T(8,128)(2,1)}, u32[]{:S(2)}) copy-start(bf16[8,272,256]{2,1,0:T(8,128)(2,1)} %copy-done.3) | copy-start | bytes 3342340
  58.4 15.3 %collective-permute-start.2 = (bf16[2,272,256]{2,1,0:T(8,128)(2,1)}, bf16[2,272,256]{2,1,0:T(8,128)(2,1)}, u32[]{:S(2)}, u32[]{:S(2)}) collective-permute-start(bf16[2,272,256]{2,1,0:T(8,128)(2,1)} %get-tuple-element.44), channel_id=1, source_target_pairs={{0,8},{2,10},{4,12},{6,14},{8,0},{10,2},{12,4},{14,6},{16,24},{18,... | collective-permute-start | bytes 835592 | tf_op jit(solution)/shard_map/ppermute | solution.py:111
  73.7 1.0 copy-start.5
  75.8 0.7 copy-start.10
  76.6 9.1 %collective-permute-start.3 = (bf16[1,272,256]{2,1,0:T(8,128)(2,1)S(1)}, bf16[1,272,256]{2,1,0:T(8,128)(2,1)S(1)}, u32[]{:S(2)}, u32[]{:S(2)}) collective-permute-start(bf16[1,272,256]{2,1,0:T(8,128)(2,1)S(1)} %get-tuple-element.46), channel_id=1, source_target_pairs={{0,16},{2,18},{4,20},{6,22},{8,24},{10,26},{12,28},{14,30},{16,0},... | collective-permute-start | bytes 417800 | tf_op jit(solution)/shard_map/ppermute | solution.py:111
  87.1 11.9 %collective-permute-start.4 = (bf16[1,256,256]{2,1,0:T(8,128)(2,1)}, bf16[1,256,256]{2,1,0:T(8,128)(2,1)}, u32[]{:S(2)}, u32[]{:S(2)}) collective-permute-start(bf16[1,256,256]{2,1,0:T(8,128)(2,1)} %get-tuple-element.25), channel_id=1, source_target_pairs={{0,16},{2,18},{4,20},{6,22},{8,24},{10,26},{12,28},{14,30},{16,0},... | collective-permute-start | bytes 393224 | tf_op jit(solution)/shard_map/ppermute | solution.py:132
  100.1 1.0 copy-start.11
  101.8 0.7 copy-start.12
  102.6 11.3 %collective-permute-start.5 = (bf16[2,256,256]{2,1,0:T(8,128)(2,1)}, bf16[2,256,256]{2,1,0:T(8,128)(2,1)}, u32[]{:S(2)}, u32[]{:S(2)}) collective-permute-start(bf16[2,256,256]{2,1,0:T(8,128)(2,1)} %get-tuple-element.28), channel_id=1, source_target_pairs={{0,8},{2,10},{4,12},{6,14},{8,0},{10,2},{12,4},{14,6},{16,24},{18,... | collective-permute-start | bytes 786440 | tf_op jit(solution)/shard_map/ppermute | solution.py:132
  113.9 34.1 %copy-start.19 = (f32[64]{0:T(128)S(1)}, f32[64]{0:T(128)}, u32[]{:S(2)}) copy-start(f32[64]{0:T(128)} %param.17) | copy-start | bytes 772
  115.2 1.1 copy-start.8
  117.2 0.8 copy-start.9
  118.0 24.3 %collective-permute-start.6 = (bf16[4,256,256]{2,1,0:T(8,128)(2,1)}, bf16[4,256,256]{2,1,0:T(8,128)(2,1)}, u32[]{:S(2)}, u32[]{:S(2)}) collective-permute-start(bf16[4,256,256]{2,1,0:T(8,128)(2,1)} %get-tuple-element.31), channel_id=1, source_target_pairs={{0,4},{2,6},{4,0},{6,2},{8,12},{10,14},{12,8},{14,10},{16,20},{18,... | collective-permute-start | bytes 1572872 | tf_op jit(solution)/shard_map/ppermute | solution.py:132
  144.1 8.1 %copy-start.13 = (f32[4096]{0:T(1024)S(1)}, f32[4096]{0:T(1024)}, u32[]{:S(2)}) copy-start(f32[4096]{0:T(1024)} %param.18) | copy-start | bytes 49156
  145.5 1.0 copy-start.6
  146.5 3.0 collective-permute-start.7
  170.4 68.4 %copy-start.17 = (f32[4096]{0:T(1024)S(1)}, f32[4096]{0:T(1024)}, u32[]{:S(2)}) copy-start(f32[4096]{0:T(1024)} %param.21) | copy-start | bytes 49156
  170.4 116.5 %copy-start.20 = (bf16[256,4096]{1,0:T(8,128)(2,1)S(1)}, bf16[256,4096]{1,0:T(8,128)(2,1)}, u32[]{:S(2)}) copy-start(bf16[256,4096]{1,0:T(8,128)(2,1)} %param.20) | copy-start | bytes 6291460
  238.9 48.1 %collective-permute-start.8 = (bf16[256,4096]{1,0:T(8,128)(2,1)}, bf16[256,4096]{1,0:T(8,128)(2,1)}, u32[]{:S(2)}, u32[]{:S(2)}) collective-permute-start(bf16[256,4096]{1,0:T(8,128)(2,1)} %convolution_convert_fusion), channel_id=1, source_target_pairs={{0,1},{1,0},{2,3},{3,2},{4,5},{5,4},{6,7},{7,6},{8,9},{9,8},{10,11... | collective-permute-start | bytes 6291464 | tf_op jit(solution)/shard_map/ppermute | solution.py:312
  304.2 1.3 copy-start.18
  305.0 1.3 copy-start.14
  306.3 47.0 %collective-permute-start.9 = (bf16[256,4096]{1,0:T(8,128)(2,1)S(1)}, bf16[256,4096]{1,0:T(8,128)(2,1)S(1)}, u32[]{:S(2)}, u32[]{:S(2)}) collective-permute-start(bf16[256,4096]{1,0:T(8,128)(2,1)S(1)} %get-tuple-element.37), channel_id=1, source_target_pairs={{0,1},{1,0},{2,3},{3,2},{4,5},{5,4},{6,7},{7,6},{8,9},{9,8},{10,11... | collective-permute-start | bytes 6291464 | tf_op jit(solution)/shard_map/ppermute | solution.py:312
  353.6 2.0 copy-start
  390.7 2.2 copy-start.1
Sparse Core Ops, SparseCore 0:
  9.5 210.9 all-gather.2
  222.1 168.5 all-gather.4

commit v4 on v3

--- a/solution.py
+++ b/solution.py
@@ -266,14 +266,17 @@
 
 def product(rows, weight):
     count, depth = rows.shape
-    columns = weight.shape[1]
-    tile = min(TILE, columns)
+    stacked = weight.ndim == 3
+    tile = weight.shape[2] if stacked else min(TILE, weight.shape[1])
+    columns = weight.shape[0] * tile if stacked else weight.shape[1]
+    by_shard = pl.BlockSpec((None, depth, tile), lambda j: (j, 0, 0))
+    by_tile = pl.BlockSpec((depth, tile), lambda j: (0, j))
     return pl.pallas_call(
         product_kernel,
         grid=(columns // tile,),
         in_specs=[
             pl.BlockSpec((count, depth), lambda j: (0, 0)),
-            pl.BlockSpec((depth, tile), lambda j: (0, j)),
+            by_shard if stacked else by_tile,
         ],
         out_specs=pl.BlockSpec((count, tile), lambda j: (0, j)),
         out_shape=jax.ShapeDtypeStruct((count, columns), jnp.bfloat16),
@@ -283,7 +286,7 @@
             bytes_accessed=2 * (count * depth + depth * columns + count * columns),
             transcendentals=0,
         ),
-        name="next_x",
+        name="product",
     )(rows, weight)
 
 
@@ -311,13 +314,13 @@
         pairs = [(i, (i + by) % head_devices) for i in range(head_devices)]
         return lax.ppermute(array, "head", pairs)
 
-    w_out_all = lax.all_gather(w_out, "seq", axis=1, tiled=True)
+    w_out_all = lax.all_gather(w_out, "seq", axis=0)
     w_in_all = lax.all_gather(w_in, "seq", axis=0, tiled=True)
     ssd_out = mixer(xin, gate_z, b_proj, c_proj, log_retain, skip_d, norm_gain, devices)
 
     def partial_of(index):
         rows = lax.dynamic_slice_in_dim(ssd_out, index * own_rows, own_rows, 0)
-        return jnp.dot(rows, w_out_all, preferred_element_type=jnp.float32).astype(jnp.bfloat16)
+        return product(rows, w_out_all)
 
     arrived = [
         shift(partial_of(lax.rem(place + by, head_devices)), by) for by in range(1, head_devices)

time: 422 us -> 405 us (0.960)
  Pallas kernels: 55.9 us -> 95.9 us
  matrix products: 35.9 us -> 0.4 us
  waiting for transfers between devices: 273 us -> 245 us
    pallas_call x1 -> x3, Pallas kernels: 21.8 us -> 64.4 us  [product(): pl.pallas_call(product_kernel, grid=(columns // tile,), in_specs=[pl.Bloc...]
    dot_general x2 -> x0, matrix products: 35.5 us -> none  [partial_of(): jnp.dot(rows, w_out_all, preferred_element_type=jnp.float32)]
    ppermute x2, waiting for transfers between devices: 93.4 us -> 69.9 us  [shift(): return lax.ppermute(array, 'head', pairs)]
    all_gather x1, waiting for transfers between devices: 50.1 us -> 28.4 us  [body(): w_out_all = lax.all_gather(w_out, 'seq', axis=0)]
    all_gather x1, waiting for transfers between devices: 35 us -> 41.6 us  [body(): w_in_all = lax.all_gather(w_in, 'seq', axis=0, tiled=True)]
    ppermute x4, waiting for transfers between devices: 44 us -> 50.2 us  [exchange(): received = lax.ppermute(theirs, 'seq', pairs)]
    unnamed x44 -> x42, local copies, waits for them, and re-layouts: 14.5 us -> 14.3 us
  transfers between devices with their start and end apart: 12 -> 12, of which waited for: 12 -> 12; matrix products, arithmetic and copies ran while one was open for 13% -> 6% of each run, Pallas kernels for 8% -> 18%
where the time goes in v4:
time: 405 us; the launch traced here: 404 us
  waiting for transfers between devices  245 us (60%)
  Pallas kernels  95.9 us (24%)
  local copies, waits for them, and re-layouts  24.7 us (6%)
  between operations  15.1 us (4%)
  other arithmetic  13.1 us (3%)
  starting transfers between devices  10.4 us (3%)
    ppermute x2, waiting for transfers between devices, shift(): return lax.ppermute(array, 'head', pairs)  69.9 us
    pallas_call x3, Pallas kernels, product(): pl.pallas_call(product_kernel, grid=(columns // tile,), in_specs=[pl.Bloc...  64.4 us
    ppermute x4, waiting for transfers between devices, exchange(): other = lax.ppermute(away, 'seq', pairs)  53 us
    ppermute x4, waiting for transfers between devices, exchange(): received = lax.ppermute(theirs, 'seq', pairs)  50.2 us
    all_gather x1, waiting for transfers between devices, body(): w_in_all = lax.all_gather(w_in, 'seq', axis=0, tiled=True)  41.6 us
    all_gather x1, waiting for transfers between devices, body(): w_out_all = lax.all_gather(w_out, 'seq', axis=0)  28.4 us
    pallas_call x1, Pallas kernels, mixer(): pl.pallas_call(functools.partial(output_kernel, blocks, width), grid=(gro...  17.9 us
    unnamed x42, local copies, waits for them, and re-layouts  14.3 us
  transfers between devices with their start and end apart: 12, of which 12 were waited for; matrix products, arithmetic and copies ran while one was open for 6% of the time, Pallas kernels for 18%

profile of v4, /device:TPU:0, one launch (start us, length us, event | category | flops | bytes accessed | tf_op | source)
XLA Modules:
  0.0 404.1 jit_solution(9850557973016225912)
XLA Ops:
  7.2 0.7 all-gather.6.cloned.1.call-update
  8.0 0.7 all-gather.4.cloned.1.call-update
  8.7 0.4 fusion.3
  9.1 0.1 copy.15
  9.2 0.1 reshape.83
  9.3 0.3 copy.17.cum_ref
  9.7 0.2 copy.19
  9.9 7.7 %block_states.1 = (bf16[16,272,256]{2,1,0:T(8,128)(2,1)}, bf16[1,256,4096]{2,1,0:T(8,128)(2,1)S(1)}) custom-call(bf16[512,4096]{1,0:T(8,128)(2,1)} %x_ref.3, bf16[512,1024]{1,0:T(8,128)(2,1)S(1)} %bitcast.34, f32[4,512,16]{2,1,0:T(8,128)S(1)} %copy.17.cum_ref), custom_call_target="tpu_custom_call" | custom-call | tf_op jit(solution)/shard_map/block_states/pallas_call | solution.py:211
  17.7 3.9 constant_dynamic-slice_fusion.8
  21.6 0.5 collective-permute-start
  22.1 2.7 collective-permute-done.other_ref
  24.8 2.0 pair_1.1
  26.8 1.0 copy-done.4
  27.8 0.9 constant_dynamic-slice_fusion.6
  28.7 2.7 collective-permute-start.1
  31.4 25.4 %collective-permute-done.1.other_ref = bf16[4,272,256]{2,1,0:T(8,128)(2,1)S(1)} collective-permute-done((bf16[4,272,256]{2,1,0:T(8,128)(2,1)}, bf16[4,272,256]{2,1,0:T(8,128)(2,1)S(1)}, u32[]{:S(2)}, u32[]{:S(2)}) %collective-permute-start.1) | collective-permute-done | bytes 557088 | tf_op jit(solution)/shard_map/ppermute | solution.py:111
  56.8 0.4 pair_2.1
  57.2 0.7 copy-done.7
  58.0 15.0 %collective-permute-done.2.other_ref = bf16[2,272,256]{2,1,0:T(8,128)(2,1)S(1)} collective-permute-done((bf16[2,272,256]{2,1,0:T(8,128)(2,1)S(1)}, bf16[2,272,256]{2,1,0:T(8,128)(2,1)S(1)}, u32[]{:S(2)}, u32[]{:S(2)}) %collective-permute-start.2) | collective-permute-done | bytes 278560 | tf_op jit(solution)/shard_map/ppermute | solution.py:111
  73.0 0.2 pair_4.1
  73.2 2.6 collective-permute-start.3
  75.8 9.9 %collective-permute-done.3.other_ref = bf16[1,272,256]{2,1,0:T(8,128)(2,1)S(1)} collective-permute-done((bf16[1,272,256]{2,1,0:T(8,128)(2,1)S(1)}, bf16[1,272,256]{2,1,0:T(8,128)(2,1)S(1)}, u32[]{:S(2)}, u32[]{:S(2)}) %collective-permute-start.3) | collective-permute-done | bytes 139296 | tf_op jit(solution)/shard_map/ppermute | solution.py:111
  85.7 0.7 pair_8.1
  86.5 0.1 collective-permute-start.4
  86.6 11.6 %collective-permute-done.4 = bf16[1,256,256]{2,1,0:T(8,128)(2,1)S(1)} collective-permute-done((bf16[1,256,256]{2,1,0:T(8,128)(2,1)S(1)}, bf16[1,256,256]{2,1,0:T(8,128)(2,1)S(1)}, u32[]{:S(2)}, u32[]{:S(2)}) %collective-permute-start.4) | collective-permute-done | bytes 131104 | tf_op jit(solution)/shard_map/ppermute | solution.py:132
  98.3 0.1 split_4.1
  98.4 0.7 copy-done.10
  99.1 13.7 %collective-permute-done.5 = bf16[2,256,256]{2,1,0:T(8,128)(2,1)S(1)} collective-permute-done((bf16[2,256,256]{2,1,0:T(8,128)(2,1)S(1)}, bf16[2,256,256]{2,1,0:T(8,128)(2,1)S(1)}, u32[]{:S(2)}, u32[]{:S(2)}) %collective-permute-start.5) | collective-permute-done | bytes 262176 | tf_op jit(solution)/shard_map/ppermute | solution.py:132
  112.9 0.7 copy-done.15
  113.6 1.4 maximum_select_fusion.2
  115.0 1.0 copy-done.8
  116.0 1.0 split_2.1
  117.0 0.8 copy-done.9
  117.8 1.6 collective-permute-start.6
  119.4 23.5 %collective-permute-done.6 = bf16[4,256,256]{2,1,0:T(8,128)(2,1)} collective-permute-done((bf16[4,256,256]{2,1,0:T(8,128)(2,1)}, bf16[4,256,256]{2,1,0:T(8,128)(2,1)}, u32[]{:S(2)}, u32[]{:S(2)}) %collective-permute-start.6) | collective-permute-done | bytes 524320 | tf_op jit(solution)/shard_map/ppermute | solution.py:132
  142.9 1.8 maximum_select_fusion.1
  144.7 1.4 split_1.1
  146.1 1.0 copy-done.6
  147.1 1.5 copy.20
  148.5 0.1 broadcast_in_dim.26
  148.6 0.1 broadcast_in_dim_reshape.3.skip_ref
  148.7 1.3 collective-permute-done.7
  150.1 2.8 maximum_select_fusion
  152.8 17.9 %mixer_out.1 = bf16[512,4096]{1,0:T(8,128)(2,1)} custom-call(bf16[512,4096]{1,0:T(8,128)(2,1)} %x_ref.3, bf16[512,4096]{1,0:T(8,128)(2,1)} %z_ref.1, bf16[512,1024]{1,0:T(8,128)(2,1)S(1)} %bitcast.35, bf16[512,1024]{1,0:T(8,128)(2,1)S(1)} %bitcast.37, f32[4,512,16]{2,1,0:T(8,128)S(1)} %copy.17.cum_ref, f32[4,16,512]{2,1,0:T(8,128)S(1)} %bitcast.41, ...), custom_call_target="tpu_custom_call" | custom-call | tf_op jit(solution)/shard_map/mixer_out/pallas_call | solution.py:228
  170.8 4.1 %constant_dynamic-slice_fusion.1 = (bf16[256,4096]{1,0:T(8,128)(2,1)S(1)}, bf16[256,4096]{1,0:T(8,128)(2,1)}) fusion(bf16[512,4096]{1,0:T(8,128)(2,1)} %mixer_out.1, s32[]{:T(128)S(6)} %select_n.120, s32[]{:T(128)S(6)} %select_n.121), kind=kLoop, calls=%fused_computation.23 | loop fusion | bytes 8388616 | tf_op jit(solution)/shard_map/dynamic_slice | solution.py:322
  174.8 28.4 %all-gather.6.cloned.1.call-done = bf16[65536,256]{1,0:T(8,128)(2,1)} async-done(((bf16[4096,256]{1,0:T(8,128)(2,1)}), bf16[65536,256]{1,0:T(8,128)(2,1)}) %all-gather.6.cloned.1.call-update) | async-done | bytes 33554448 | tf_op jit(solution)/shard_map/all_gather | solution.py:317
  203.2 1.6 copy-done
  204.8 21.6 %product.4 = bf16[256,4096]{1,0:T(8,128)(2,1)} custom-call(bf16[256,4096]{1,0:T(8,128)(2,1)S(1)} %copy-done, bf16[16,4096,256]{2,1,0:T(8,128)(2,1)} %bitcast.46), custom_call_target="tpu_custom_call" | custom-call | flops 8589934592 | bytes 37748736 | tf_op jit(solution)/shard_map/product/pallas_call | solution.py:274
  226.5 1.4 collective-permute-start.8
  227.9 0.6 multiply_reduce_fusion.1
  229.2 20.9 %product.3 = bf16[256,4096]{1,0:T(8,128)(2,1)S(1)} custom-call(bf16[256,4096]{1,0:T(8,128)(2,1)S(1)} %get-tuple-element.40.rows_ref, bf16[16,4096,256]{2,1,0:T(8,128)(2,1)} %bitcast.47), custom_call_target="tpu_custom_call" | custom-call | flops 8589934592 | bytes 37748736 | tf_op jit(solution)/shard_map/product/pallas_call | solution.py:274
  250.2 24.4 %collective-permute-done.8 = bf16[256,4096]{1,0:T(8,128)(2,1)} collective-permute-done((bf16[256,4096]{1,0:T(8,128)(2,1)}, bf16[256,4096]{1,0:T(8,128)(2,1)}, u32[]{:S(2)}, u32[]{:S(2)}) %collective-permute-start.8) | collective-permute-done | bytes 2097184 | tf_op jit(solution)/shard_map/ppermute | solution.py:315
  274.5 2.6 multiply_reduce_fusion
  277.2 3.1 fusion
  280.4 0.5 broadcast_in_dim.29
  280.9 0.8 copy-done.13
  281.6 0.8 constant_dynamic-update-slice_fusion.1
  282.4 1.5 collective-permute-start.9
  283.9 45.5 %collective-permute-done.9 = bf16[256,4096]{1,0:T(8,128)(2,1)S(1)} collective-permute-done((bf16[256,4096]{1,0:T(8,128)(2,1)S(1)}, bf16[256,4096]{1,0:T(8,128)(2,1)S(1)}, u32[]{:S(2)}, u32[]{:S(2)}) %collective-permute-start.9) | collective-permute-done | bytes 2097184 | tf_op jit(solution)/shard_map/ppermute | solution.py:315
  329.4 0.3 constant_dynamic-update-slice_fusion.rows_ref
  329.7 2.0 copy-done.1
  331.7 41.6 %all-gather.4.cloned.1.call-done.weight_ref = bf16[4096,4096]{1,0:T(8,128)(2,1)} async-done(((bf16[256,4096]{1,0:T(8,128)(2,1)}), bf16[4096,4096]{1,0:T(8,128)(2,1)}) %all-gather.4.cloned.1.call-update) | async-done | bytes 33554448 | tf_op jit(solution)/shard_map/all_gather | solution.py:318
  373.3 2.2 copy-done.2
  375.5 21.8 %product.5 = bf16[512,4096]{1,0:T(8,128)(2,1)} custom-call(bf16[512,4096]{1,0:T(8,128)(2,1)S(1)} %copy-done.2, bf16[4096,4096]{1,0:T(8,128)(2,1)} %all-gather.4.cloned.1.call-done.weight_ref), custom_call_target="tpu_custom_call" | custom-call | flops 17179869184 | bytes 41943040 | tf_op jit(solution)/shard_map/product/pallas_call | solution.py:274
  (42 shorter events, 0.4 us)
Async XLA Ops:
  7.2 1.5 copy-start.16
  7.2 196.1 %all-gather.6.cloned.1.call-start = ((), (), s32[]{:S(2)}) async-start(), calls=%async_computation.1 | async-start | bytes 35651584 | tf_op jit(solution)/shard_map/all_gather | solution.py:317
  7.9 1.8 copy-start.14
  7.9 365.4 %all-gather.4.cloned.1.call-start = ((), (), s32[]{:S(2)}) async-start(), calls=%async_computation | async-start | bytes 35651584 | tf_op jit(solution)/shard_map/all_gather | solution.py:318
  17.7 3.9 copy-start.3
  21.6 3.2 collective-permute-start
  26.8 1.0 copy-start.4
  28.7 28.1 %collective-permute-start.1 = (bf16[4,272,256]{2,1,0:T(8,128)(2,1)}, bf16[4,272,256]{2,1,0:T(8,128)(2,1)S(1)}, u32[]{:S(2)}, u32[]{:S(2)}) collective-permute-start(bf16[4,272,256]{2,1,0:T(8,128)(2,1)} %get-tuple-element.44), channel_id=1, source_target_pairs={{0,4},{2,6},{4,0},{6,2},{8,12},{10,14},{12,8},{14,10},{16,20},{18,... | collective-permute-start | bytes 1671176 | tf_op jit(solution)/shard_map/ppermute | solution.py:111
  57.1 0.8 copy-start.7
  57.9 15.0 %collective-permute-start.2 = (bf16[2,272,256]{2,1,0:T(8,128)(2,1)S(1)}, bf16[2,272,256]{2,1,0:T(8,128)(2,1)S(1)}, u32[]{:S(2)}, u32[]{:S(2)}) collective-permute-start(bf16[2,272,256]{2,1,0:T(8,128)(2,1)S(1)} %get-tuple-element.46), channel_id=1, source_target_pairs={{0,8},{2,10},{4,12},{6,14},{8,0},{10,2},{12,4},{14,6},{16,24},{18,... | collective-permute-start | bytes 835592 | tf_op jit(solution)/shard_map/ppermute | solution.py:111
  73.2 12.5 %collective-permute-start.3 = (bf16[1,272,256]{2,1,0:T(8,128)(2,1)S(1)}, bf16[1,272,256]{2,1,0:T(8,128)(2,1)S(1)}, u32[]{:S(2)}, u32[]{:S(2)}) collective-permute-start(bf16[1,272,256]{2,1,0:T(8,128)(2,1)S(1)} %get-tuple-element.48), channel_id=1, source_target_pairs={{0,16},{2,18},{4,20},{6,22},{8,24},{10,26},{12,28},{14,30},{16,0},... | collective-permute-start | bytes 417800 | tf_op jit(solution)/shard_map/ppermute | solution.py:111
  86.5 11.7 %collective-permute-start.4 = (bf16[1,256,256]{2,1,0:T(8,128)(2,1)S(1)}, bf16[1,256,256]{2,1,0:T(8,128)(2,1)S(1)}, u32[]{:S(2)}, u32[]{:S(2)}) collective-permute-start(bf16[1,256,256]{2,1,0:T(8,128)(2,1)S(1)} %get-tuple-element.25), channel_id=1, source_target_pairs={{0,16},{2,18},{4,20},{6,22},{8,24},{10,26},{12,28},{14,30},{16,0},... | collective-permute-start | bytes 393224 | tf_op jit(solution)/shard_map/ppermute | solution.py:132
  98.4 0.7 copy-start.10
  99.1 13.8 %collective-permute-start.5 = (bf16[2,256,256]{2,1,0:T(8,128)(2,1)S(1)}, bf16[2,256,256]{2,1,0:T(8,128)(2,1)S(1)}, u32[]{:S(2)}, u32[]{:S(2)}) collective-permute-start(bf16[2,256,256]{2,1,0:T(8,128)(2,1)S(1)} %get-tuple-element.28), channel_id=1, source_target_pairs={{0,8},{2,10},{4,12},{6,14},{8,0},{10,2},{12,4},{14,6},{16,24},{18,... | collective-permute-start | bytes 786440 | tf_op jit(solution)/shard_map/ppermute | solution.py:132
  112.9 0.7 copy-start.15
  113.6 31.1 %copy-start.5 = (bf16[8,272,256]{2,1,0:T(8,128)(2,1)S(1)}, bf16[8,272,256]{2,1,0:T(8,128)(2,1)}, u32[]{:S(2)}) copy-start(bf16[8,272,256]{2,1,0:T(8,128)(2,1)} %copy-done.4) | copy-start | bytes 3342340
  115.0 1.1 copy-start.8
  117.0 0.8 copy-start.9
  117.8 25.1 %collective-permute-start.6 = (bf16[4,256,256]{2,1,0:T(8,128)(2,1)}, bf16[4,256,256]{2,1,0:T(8,128)(2,1)}, u32[]{:S(2)}, u32[]{:S(2)}) collective-permute-start(bf16[4,256,256]{2,1,0:T(8,128)(2,1)} %get-tuple-element.31), channel_id=1, source_target_pairs={{0,4},{2,6},{4,0},{6,2},{8,12},{10,14},{12,8},{14,10},{16,20},{18,... | collective-permute-start | bytes 1572872 | tf_op jit(solution)/shard_map/ppermute | solution.py:132
  144.7 3.9 copy-start.19
  146.1 1.0 copy-start.6
  147.1 3.0 collective-permute-start.7
  150.1 2.8 copy-start.11
  203.2 1.6 copy-start
  204.8 23.1 %copy-start.17 = (f32[4096]{0:T(1024)S(1)}, f32[4096]{0:T(1024)}, u32[]{:S(2)}) copy-start(f32[4096]{0:T(1024)} %param.21) | copy-start | bytes 49156
  226.5 48.1 %collective-permute-start.8 = (bf16[256,4096]{1,0:T(8,128)(2,1)}, bf16[256,4096]{1,0:T(8,128)(2,1)}, u32[]{:S(2)}, u32[]{:S(2)}) collective-permute-start(bf16[256,4096]{1,0:T(8,128)(2,1)} %product.4), channel_id=1, source_target_pairs={{0,1},{1,0},{2,3},{3,2},{4,5},{5,4},{6,7},{7,6},{8,9},{9,8},{10,11... | collective-permute-start | bytes 6291464 | tf_op jit(solution)/shard_map/ppermute | solution.py:315
  229.2 45.3 %copy-start.12 = (bf16[256,4096]{1,0:T(8,128)(2,1)S(1)}, bf16[256,4096]{1,0:T(8,128)(2,1)}, u32[]{:S(2)}) copy-start(bf16[256,4096]{1,0:T(8,128)(2,1)} %param.20) | copy-start | bytes 6291460
  280.3 1.3 copy-start.13
  280.3 1.3 copy-start.18
  282.4 47.0 %collective-permute-start.9 = (bf16[256,4096]{1,0:T(8,128)(2,1)S(1)}, bf16[256,4096]{1,0:T(8,128)(2,1)S(1)}, u32[]{:S(2)}, u32[]{:S(2)}) collective-permute-start(bf16[256,4096]{1,0:T(8,128)(2,1)S(1)} %get-tuple-element.37), channel_id=1, source_target_pairs={{0,1},{1,0},{2,3},{3,2},{4,5},{5,4},{6,7},{7,6},{8,9},{9,8},{10,11... | collective-permute-start | bytes 6291464 | tf_op jit(solution)/shard_map/ppermute | solution.py:315
  329.7 2.0 copy-start.1
  373.3 2.2 copy-start.2
Sparse Core Ops, SparseCore 0:
  9.6 193.5 all-gather.5
  204.8 168.4 all-gather.3
